TPU v7x, 512 devices: a whole 4x8x8 slice. The times are simulated.
512 devices in a mesh: redist: 64 (over z, y), contract: 8 (over x, core).
Axes of the slice: x: 4, y: 8, z: 8, core: 2. Of those that a mesh axis runs over, the one named last changes fastest.
Arguments:
- amplitudes: float32 [512, 8, 16384], P('redist', 'contract'), may hold values from -6 to 6
- integrals: float32 [8, 16384, 512], P('contract', 'redist'), may hold values from -0.0390625 to 0.0390625
- irrep_count: int32 [8], replicated, may hold values from 1 to 128, 900 in all
- pair_energy: float32 [512], P(('redist', 'contract')), may hold values from -2 to -0.5
- virt_energy: float32 [512], replicated, may hold values from 1 to 3
Outputs:
- delta: float32 [512, 512], P(('redist', 'contract'))
Inputs may be any that keep to these rules, and one draw needn't show every extreme that they name: irrep_count[h] counts the virtual orbitals of irrep h; the counts sum to 900 and the largest is exactly 128.
All inputs are finite; a program needn't handle non-finite values.
Results may differ from a plain program's by a relative error of at most 0.0001.
Values sent between devices are 32-bit elements; how exact they have to be, the bound alone decides.
No kernel may reach another device: no remote copies, remote signals or barrier semaphores. Data moves between devices by JAX's collectives and lax.ppermute only.
A program may use at most 64 MiB of HBM per device.

v0:
```python
import jax
import jax.numpy as jnp
from jax import lax
from jax.sharding import PartitionSpec as P

VMAX = 128
GAMMA = 3


def live_mask(irrep_count, first_irrep, irrep_total, first_cell, cell_count):
    irreps = first_irrep + jnp.arange(irrep_total, dtype=jnp.int32)
    partner = jnp.bitwise_xor(irreps, GAMMA)
    irrep_table = jnp.arange(irrep_count.shape[0], dtype=jnp.int32)
    own_count = jnp.sum(
        jnp.where(irrep_table[None, :] == irreps[:, None], irrep_count[None, :], 0), axis=1
    )
    partner_count = jnp.sum(
        jnp.where(irrep_table[None, :] == partner[:, None], irrep_count[None, :], 0), axis=1
    )
    cell_index = first_cell + jnp.arange(cell_count, dtype=jnp.int32)
    row_index = cell_index // VMAX
    col_index = cell_index % VMAX
    return (
        (row_index[None, :] < own_count[:, None]) & (col_index[None, :] < partner_count[:, None])
    ).astype(jnp.float32)


def make_term(source, weights):
    return jnp.dot(
        source, weights, precision=lax.Precision.HIGHEST, preferred_element_type=jnp.float32
    )


def body(amplitudes, integrals, irrep_count, pair_energy, virt_energy):
    slab_devices = lax.axis_size("redist")
    pair_dev, irr_dev, cells_all = amplitudes.shape
    cell_count = integrals.shape[1]
    virt_pairs = integrals.shape[2]
    first_cell = lax.axis_index("redist") * cell_count
    live = live_mask(
        irrep_count, lax.axis_index("contract") * irr_dev, irr_dev, first_cell, cell_count
    )
    weights = (integrals * (0.5 * live)[:, :, None]).reshape(irr_dev * cell_count, virt_pairs)
    arrived = lax.all_to_all(amplitudes, "redist", split_axis=2, concat_axis=0, tiled=True)
    rows_all = arrived.reshape(pair_dev * slab_devices, irr_dev * cell_count)
    ladder = lax.psum_scatter(
        make_term(rows_all, weights), ("redist", "contract"), scatter_dimension=0, tiled=True
    )
    return ladder / (virt_energy[None, :] - pair_energy[:, None])


def solution(mesh):
    in_specs = (
        P("redist", "contract", None),
        P("contract", "redist", None),
        P(),
        P(("redist", "contract")),
        P(),
    )
    out_specs = P(("redist", "contract"), None)
    return jax.shard_map(body, mesh=mesh, in_specs=in_specs, out_specs=out_specs, check_vma=False)
```

profile of v0, /device:TPU:1, one launch (start us, length us, event | category | flops | bytes accessed | tf_op | source)
XLA Modules:
  0.0 441.1 jit_solution(16779044277024733189)
XLA Ops:
  6.5 15.0 %copy.16 = f32[8,1,16384]{0,1,2:T(1,128)} copy(f32[8,1,16384]{2,1,0:T(1,128)} %param.5) | data formatting | bytes 1048576 | tf_op args[0]
  21.5 0.5 broadcast.117
  22.1 74.5 %reduce.4 = f32[16384,8]{1,0:T(8,128)} reduce(f32[16384,1,8]{2,1,0:T(1,128)} %bitcast.17, f32[]{:T(128)} %broadcast.117), dimensions={1}, to_apply=%bitcast.14.reduce_sub_computation | reduce | bytes 1048580
  96.5 0.0 copy-start.2
  96.5 7.4 %reshape.81 = f32[64,1,2048]{2,1,0:T(1,128)} reshape(f32[16384,8]{1,0:T(8,128)} %reduce.4) | data formatting | bytes 1048576
  104.0 17.1 %all-to-all-start = ((f32[64,1,2048]{2,1,0:T(1,128)}), f32[64,1,2048]{2,1,0:T(1,128)S(1)}, u32[]{:S(2)}, u32[]{:S(2)}) async-start(f32[64,1,2048]{2,1,0:T(1,128)} %reshape.81), calls=%async_computation | async-start | bytes 1048576 | tf_op jit(solution)/shard_map/all_to_all | solution.py:44
  121.1 0.2 all-reduce.3.cloned.1.call-start
  121.3 0.0 copy-done.2
  121.3 0.7 fusion.5
  122.1 1.3 and_select_fusion
  123.3 14.9 %all-to-all-done = f32[64,1,2048]{2,1,0:T(1,128)S(1)} async-done(((f32[64,1,2048]{2,1,0:T(1,128)}), f32[64,1,2048]{2,1,0:T(1,128)S(1)}, u32[]{:S(2)}, u32[]{:S(2)}) %all-to-all-start) | async-done | bytes 524320 | tf_op jit(solution)/shard_map/all_to_all | solution.py:44
  138.3 1.9 reduce.5
  140.2 0.0 copy-start
  140.2 0.0 copy-start.1
  140.2 15.4 %reshape.82 = f32[16384,1,8]{2,1,0:T(1,128)} reshape(f32[64,2048]{1,0:T(8,128)S(1)} %reduce.5) | data formatting | bytes 1048576
  155.6 5.2 %copy.20 = f32[8,1,64,256]{3,2,0,1:T(8,128)S(1)} copy(f32[8,1,64,256]{0,3,2,1:T(8,128)} %bitcast.18) | data formatting | bytes 1048576 | tf_op jit(solution)/shard_map/all_to_all | solution.py:44
  160.8 0.0 copy-done
  160.8 3.0 convolution_bitcast_fusion
  163.8 0.0 all-reduce.3.cloned.1.call-update
  164.5 0.0 copy-done.1
  164.5 268.0 %all-reduce.3.cloned.1.call-done = f32[512,512]{0,1:T(8,128)} async-done(((f32[512,512]{0,1:T(8,128)}), f32[512,512]{0,1:T(8,128)}) %all-reduce.3.cloned.1.call-update) | async-done | bytes 1048592
  432.5 1.1 constant_dynamic-slice_fusion
  433.6 0.1 copy.19
  433.7 0.6 div.19
  (1 shorter events, 0.0 us)
Async XLA Ops:
  96.5 24.8 %copy-start.2 = (s32[8]{0:T(128)S(1)}, s32[8]{0:T(128)}, u32[]{:S(2)}) copy-start(s32[8]{0:T(128)} %param.7) | copy-start | bytes 100
  104.0 34.3 %all-to-all-start = ((f32[64,1,2048]{2,1,0:T(1,128)}), f32[64,1,2048]{2,1,0:T(1,128)S(1)}, u32[]{:S(2)}, u32[]{:S(2)}) async-start(f32[64,1,2048]{2,1,0:T(1,128)} %reshape.81), calls=%async_computation | async-start | bytes 1048576 | tf_op jit(solution)/shard_map/all_to_all | solution.py:44
  121.1 311.4 %all-reduce.3.cloned.1.call-start = ((), (), s32[]{:S(2)}) async-start(), calls=%async_computation.1 | async-start | bytes 2097152
  140.2 20.6 %copy-start = (f32[1,256,512]{2,1,0:T(8,128)S(1)}, f32[1,256,512]{2,1,0:T(8,128)}, u32[]{:S(2)}) copy-start(f32[1,256,512]{2,1,0:T(8,128)} %param.6) | copy-start | bytes 1572868
  140.2 24.3 %copy-start.1 = (f32[512]{0:T(512)S(1)}, f32[512]{0:T(512)}, u32[]{:S(2)}) copy-start(f32[512]{0:T(512)} %param.9) | copy-start | bytes 6148
Sparse Core Ops, SparseCore 0:
  164.0 268.4 all-reduce.2
where the time goes:
time: 443 us; the launch traced here: 441 us
  waiting for transfers between devices  283 us (64%)
  other arithmetic  78.9 us (18%)
  local copies, waits for them, and re-layouts  44.7 us (10%)
  starting transfers between devices  17.4 us (4%)
  between operations  14.1 us (3%)
    unnamed x2, waiting for transfers between devices  268 us
    unnamed x1, other arithmetic  74.5 us
    unnamed x11, local copies, waits for them, and re-layouts  39.5 us
    all_to_all x1, starting transfers between devices, body(): lax.all_to_all(amplitudes, 'redist', split_axis=2, concat_axis=0, tiled=T...  17.1 us
    all_to_all x1, waiting for transfers between devices, body(): lax.all_to_all(amplitudes, 'redist', split_axis=2, concat_axis=0, tiled=T...  14.9 us
  transfers between devices with their start and end apart: 2, of which 2 were waited for; matrix products, arithmetic and copies ran while one was open for 0% of the time, Pallas kernels for 0%

commit v1 on v0

v1 whole, which is shorter than its diff:
```python
import jax
import jax.numpy as jnp
from jax import lax
from jax.experimental import pallas as pl
from jax.experimental.pallas import tpu as pltpu
from jax.sharding import PartitionSpec as P

VMAX = 128
GAMMA = 3
VMEM_BYTES = 48 * 1024 * 1024


def regroup_kernel(cells_ref, out_ref):
    pairs, _, _ = cells_ref.shape
    slabs, lines, _ = out_ref.shape
    parts = lines // pairs
    for pair in range(pairs):
        for part in range(parts):
            out_ref[:, pair * parts + part, :] = cells_ref[pair, pl.ds(part, slabs, stride=parts), :]


def split_bf16(value):
    high = value.astype(jnp.bfloat16)
    return high, (value - high.astype(jnp.float32)).astype(jnp.bfloat16)


def ladder_kernel(count_ref, rows_ref, integrals_ref, out_ref):
    pairs, slabs, _ = out_ref.shape
    lines = rows_ref.shape[1]
    parts = lines // pairs
    irrep = lax.axis_index("contract")
    first_row = lax.axis_index("redist") * parts
    own_count = count_ref[irrep]
    partner_count = count_ref[jnp.bitwise_xor(irrep, GAMMA)]
    cells, _ = integrals_ref.shape
    cell = lax.broadcasted_iota(jnp.int32, integrals_ref.shape, 0)
    live = (first_row + cell // VMAX < own_count) & (cell % VMAX < partner_count)
    weights = jnp.where(live, 0.5 * integrals_ref[...], 0.0)
    rows = jnp.concatenate(
        [
            jnp.concatenate([rows_ref[:, pair * parts + part, :] for part in range(parts)], axis=1)
            for pair in range(pairs)
        ],
        axis=0,
    )
    total = jnp.dot(
        rows, weights, precision=lax.Precision.HIGHEST, preferred_element_type=jnp.float32
    )
    out_ref[...] = total.reshape(out_ref.shape)


def contract_sum_kernel(parts_ref, out_ref):
    total = jnp.sum(parts_ref[...], axis=0)
    slabs = total.shape[0]
    blocks = total.shape[1] // 128
    for block in range(blocks):
        out_ref[pl.ds(block, slabs, stride=blocks), :] = total[:, block * 128 : (block + 1) * 128]


def finish_kernel(pair_energy_ref, parts_ref, virt_energy_ref, out_ref):
    blocks = out_ref.shape[0]
    slabs = parts_ref.shape[0] // blocks
    total = jnp.concatenate(
        [
            jnp.sum(parts_ref[pl.ds(block, slabs, stride=blocks), :], axis=0, keepdims=True)
            for block in range(blocks)
        ],
        axis=0,
    )
    out_ref[...] = total / (virt_energy_ref[...] - pair_energy_ref[0])


def call(kernel, out_shape, in_memory):
    return pl.pallas_call(
        kernel,
        out_shape=jax.ShapeDtypeStruct(out_shape, jnp.float32),
        in_specs=[pl.BlockSpec(memory_space=space) for space in in_memory],
        out_specs=pl.BlockSpec(memory_space=pltpu.VMEM),
        compiler_params=pltpu.CompilerParams(vmem_limit_bytes=VMEM_BYTES),
    )


def body(amplitudes, integrals, irrep_count, pair_energy, virt_energy):
    slabs = lax.axis_size("redist")
    owners = lax.axis_size("contract")
    pairs, _, cells_all = amplitudes.shape
    _, cells, virt = integrals.shape
    parts = cells // VMAX
    vmem, smem = pltpu.VMEM, pltpu.SMEM

    grouped = call(regroup_kernel, (slabs, pairs * parts, VMAX), [vmem])(
        amplitudes.reshape(pairs, cells_all // VMAX, VMAX)
    )
    arrived = lax.all_to_all(grouped, "redist", split_axis=0, concat_axis=0, tiled=True)
    partial = call(ladder_kernel, (owners, slabs, virt), [smem, vmem, vmem])(
        irrep_count, arrived, integrals.reshape(cells, virt)
    )
    partial = lax.all_to_all(partial, "contract", split_axis=0, concat_axis=0, tiled=True)
    blocks = virt // 128
    summed = call(contract_sum_kernel, (slabs * blocks, 128), [vmem])(partial)
    summed = lax.all_to_all(
        summed.reshape(slabs, blocks, 128), "redist", split_axis=0, concat_axis=0, tiled=True
    )
    delta = call(finish_kernel, (blocks, 128), [smem, vmem, vmem])(
        pair_energy, summed.reshape(slabs * blocks, 128), virt_energy.reshape(blocks, 128)
    )
    return delta.reshape(1, virt)


def solution(mesh):
    in_specs = (
        P("redist", "contract", None),
        P("contract", "redist", None),
        P(),
        P(("redist", "contract")),
        P(),
    )
    out_specs = P(("redist", "contract"), None)
    return jax.shard_map(body, mesh=mesh, in_specs=in_specs, out_specs=out_specs, check_vma=False)
```

time: 443 us -> 78.9 us (0.18)
  waiting for transfers between devices: 283 us -> 10.9 us
  other arithmetic: 78.9 us -> 0 us
  blocking collectives: 0 us -> 56.9 us
  local copies, waits for them, and re-layouts: 44.7 us -> 1.71 us
  between operations: 14.1 us -> 0.69 us
  starting transfers between devices: 17.4 us -> 4.72 us
    unnamed x2 -> x0, waiting for transfers between devices: 268 us -> none
    unnamed x1 -> x0, other arithmetic: 74.5 us -> none
    all_to_all x0 -> x2, blocking collectives: none -> 56.9 us  [the longest x1 34.2 us: body(): lax.all_to_all(grouped, 'redist', split_axis=0, concat_axis=0, tiled=True)]
    unnamed x11 -> x8, local copies, waits for them, and re-layouts: 39.5 us -> 1.71 us
    all_to_all x1, starting transfers between devices: 17.1 us -> 4.72 us  [body(): lax.all_to_all(summed.reshape(slabs, blocks, 128), 'redist', split_axis=0...]
    all_to_all x1 -> x0, local copies, waits for them, and re-layouts: 5.15 us -> none  [body(): lax.all_to_all(amplitudes, 'redist', split_axis=2, concat_axis=0, tiled=T...]
  transfers between devices with their start and end apart: 2 -> 1, of which waited for: 2 -> 1; matrix products, arithmetic and copies ran while one was open for 0% -> 0% of each run, Pallas kernels for 0% -> 0%
where the time goes in v1:
time: 78.9 us; the launch traced here: 78.4 us
  blocking collectives  56.9 us (72%)
  waiting for transfers between devices  10.9 us (14%)
  starting transfers between devices  4.72 us (6%)
  Pallas kernels  3.5 us (4%)
  local copies, waits for them, and re-layouts  1.71 us (2%)
    all_to_all x1, blocking collectives, body(): lax.all_to_all(grouped, 'redist', split_axis=0, concat_axis=0, tiled=True)  34.2 us
    all_to_all x1, blocking collectives, body(): lax.all_to_all(partial, 'contract', split_axis=0, concat_axis=0, tiled=True)  22.7 us
    all_to_all x1, waiting for transfers between devices, body(): lax.all_to_all(summed.reshape(slabs, blocks, 128), 'redist', split_axis=0...  10.9 us
    all_to_all x1, starting transfers between devices, body(): lax.all_to_all(summed.reshape(slabs, blocks, 128), 'redist', split_axis=0...  4.72 us
    pallas_call x1, Pallas kernels, body(): call(ladder_kernel, (owners, slabs, virt), [smem, vmem, vmem])  1.85 us
    unnamed x8, local copies, waits for them, and re-layouts  1.71 us
  transfers between devices with their start and end apart: 1, of which 1 were waited for; matrix products, arithmetic and copies ran while one was open for 0% of the time, Pallas kernels for 0%

profile of v1, /device:TPU:1, one launch (start us, length us, event | category | flops | bytes accessed | tf_op | source)
XLA Modules:
  0.0 78.4 jit_solution(775153115836735275)
XLA Ops:
  0.0 0.0 copy-start.1
  0.0 1.0 %copy-done.1 = f32[8,1,16384]{2,1,0:T(1,128)S(1)} copy-done((f32[8,1,16384]{2,1,0:T(1,128)S(1)}, f32[8,1,16384]{2,1,0:T(1,128)}, u32[]{:S(2)}) %copy-start.1) | copy-done | bytes 524312
  1.0 0.3 shard_map.55
  1.4 0.0 copy-start
  1.4 34.2 %all_to_all.15.rows_ref = f32[64,16,128]{2,1,0:T(8,128)S(1)} all-to-all(f32[64,16,128]{2,1,0:T(8,128)S(1)} %shard_map.55), channel_id=1, replica_groups=mesh['redist'=64,'contract'=8] {'redist'}, dimensions={0} | all-to-all | bytes 1048576 | tf_op jit(solution)/shard_map/all_to_all | solution.py:94
  35.6 0.0 copy-start.3
  35.6 0.0 copy-done
  35.6 0.7 copy-done.3
  36.3 1.9 %shard_map.56 = f32[8,64,512]{2,1,0:T(8,128)S(1)} custom-call(s32[8]{0:T(128)S(1)} %copy-done.3, f32[64,16,128]{2,1,0:T(8,128)S(1)} %all_to_all.15.rows_ref, f32[256,512]{1,0:T(8,128)S(1)} %bitcast.6), custom_call_target="tpu_custom_call" | custom-call | tf_op jit(solution)/shard_map/pallas_call | solution.py:95
  38.1 22.7 %all_to_all.16.parts_ref = f32[8,64,512]{2,1,0:T(8,128)S(1)} all-to-all(f32[8,64,512]{2,1,0:T(8,128)S(1)} %shard_map.56), channel_id=1, replica_groups=mesh['redist'=64,'contract'=8] {'contract'}, dimensions={0} | all-to-all | bytes 2097152 | tf_op jit(solution)/shard_map/all_to_all | solution.py:98
  60.8 0.7 shard_map.57
  61.5 4.7 %all-to-all-start.2 = ((f32[64,4,128]{2,1,0:T(4,128)}), f32[64,4,128]{2,1,0:T(4,128)S(1)}, u32[]{:S(2)}, u32[]{:S(2)}) async-start(f32[64,4,128]{2,1,0:T(4,128)} %bitcast.2), calls=%async_computation.2 | async-start | bytes 262144 | tf_op jit(solution)/shard_map/all_to_all | solution.py:101
  66.9 0.0 copy-start.2
  66.9 10.9 %all-to-all-done.2 = f32[64,4,128]{2,1,0:T(4,128)S(1)} async-done(((f32[64,4,128]{2,1,0:T(4,128)}), f32[64,4,128]{2,1,0:T(4,128)S(1)}, u32[]{:S(2)}, u32[]{:S(2)}) %all-to-all-start.2) | async-done | bytes 131104 | tf_op jit(solution)/shard_map/all_to_all | solution.py:101
  77.8 0.0 copy-done.2
  77.8 0.6 shard_map.58
Async XLA Ops:
  0.0 1.0 %copy-start.1 = (f32[8,1,16384]{2,1,0:T(1,128)S(1)}, f32[8,1,16384]{2,1,0:T(1,128)}, u32[]{:S(2)}) copy-start(f32[8,1,16384]{2,1,0:T(1,128)} %param.5) | copy-start | bytes 1572868
  1.4 34.3 %copy-start = (f32[1,256,512]{2,1,0:T(8,128)S(1)}, f32[1,256,512]{2,1,0:T(8,128)}, u32[]{:S(2)}) copy-start(f32[1,256,512]{2,1,0:T(8,128)} %param.6) | copy-start | bytes 1572868
  35.6 0.7 copy-start.3
  61.5 16.3 %all-to-all-start.2 = ((f32[64,4,128]{2,1,0:T(4,128)}), f32[64,4,128]{2,1,0:T(4,128)S(1)}, u32[]{:S(2)}, u32[]{:S(2)}) async-start(f32[64,4,128]{2,1,0:T(4,128)} %bitcast.2), calls=%async_computation.2 | async-start | bytes 262144 | tf_op jit(solution)/shard_map/all_to_all | solution.py:101
  66.9 10.9 %copy-start.2 = (f32[512]{0:T(512)S(1)}, f32[512]{0:T(512)}, u32[]{:S(2)}) copy-start(f32[512]{0:T(512)} %param.9) | copy-start | bytes 6148

commit v2 on v1

v2 whole, which is shorter than its diff:
```python
import jax
import jax.numpy as jnp
from jax import lax
from jax.experimental import pallas as pl
from jax.experimental.pallas import tpu as pltpu
from jax.sharding import PartitionSpec as P

VMAX = 128
GAMMA = 3
CORES = 2
CHUNKS = 4
VMEM_BYTES = 48 * 1024 * 1024


def regroup_kernel(cells_ref, out_ref, held, ready, in_sems, out_sems):
    pairs, all_lines, _ = cells_ref.shape
    slabs, lines, _ = out_ref.shape
    parts = lines // pairs
    chunks = in_sems.shape[0]
    slabs_each, lines_each = slabs // chunks, all_lines // chunks
    arrivals = [
        pltpu.make_async_copy(
            cells_ref.at[:, pl.ds(chunk * lines_each, lines_each), :],
            held.at[chunk],
            in_sems.at[chunk],
        )
        for chunk in range(chunks)
    ]
    departures = [
        pltpu.make_async_copy(
            ready.at[chunk],
            out_ref.at[pl.ds(chunk * slabs_each, slabs_each)],
            out_sems.at[chunk],
        )
        for chunk in range(chunks)
    ]
    for arrival in arrivals:
        arrival.start()
    for chunk in range(chunks):
        arrivals[chunk].wait()
        for pair in range(pairs):
            line = (pair % CORES) * (lines // CORES) + (pair // CORES) * parts
            for part in range(parts):
                ready[chunk, :, line + part, :] = held[
                    chunk, pair, pl.ds(part, slabs_each, stride=parts), :
                ]
        departures[chunk].start()
    for departure in departures:
        departure.wait()


def split_bf16(value):
    high = value.astype(jnp.bfloat16)
    return high, (value - high.astype(jnp.float32)).astype(jnp.bfloat16)


def weights_kernel(
    count_ref, pair_energy_ref, own_ref, other_ref, virt_energy_ref, high_ref, low_ref, gap_ref
):
    cells, virt = own_ref.shape
    irrep = lax.axis_index("contract")
    core = irrep % CORES
    first_row = lax.axis_index("redist") * (cells // VMAX)
    cell = lax.broadcasted_iota(jnp.int32, (cells, virt), 0)
    row, col = first_row + cell // VMAX, cell % VMAX
    for source in range(CORES):
        owner = irrep - core + source
        live = (row < count_ref[owner]) & (col < count_ref[jnp.bitwise_xor(owner, GAMMA)])
        held = jnp.where(core == source, own_ref[...], other_ref[...])
        high, low = split_bf16(jnp.where(live, 0.5 * held, 0.0))
        high_ref[pl.ds(source * cells, cells), :] = high
        low_ref[pl.ds(source * cells, cells), :] = low
    gap_ref[...] = virt_energy_ref[...] - pair_energy_ref[0]


def ladder_kernel(rows_ref, high_ref, low_ref, out_ref):
    slabs, lines, _ = rows_ref.shape
    depth, virt = high_ref.shape
    blocks = virt // VMAX
    turns = out_ref.shape[1] // blocks
    pieces = depth // VMAX
    parts = pieces // CORES
    rows = jnp.concatenate(
        [
            jnp.concatenate(
                [
                    rows_ref[:, (source * turns + turn) * parts + part, :]
                    for source in range(CORES)
                    for part in range(parts)
                ],
                axis=1,
            )
            for turn in range(turns)
        ],
        axis=0,
    )
    rows_high, rows_low = split_bf16(rows)
    high, low = high_ref[...], low_ref[...]
    total = jnp.dot(rows_high, low, preferred_element_type=jnp.float32)
    total = total + jnp.dot(rows_low, high, preferred_element_type=jnp.float32)
    total = total + jnp.dot(rows_high, high, preferred_element_type=jnp.float32)
    for turn in range(turns):
        for block in range(blocks):
            out_ref[:, turn * blocks + block, :] = total[
                turn * slabs : (turn + 1) * slabs, block * VMAX : (block + 1) * VMAX
            ]


def finish_kernel(parts_ref, gap_ref, out_ref):
    blocks = out_ref.shape[0]
    total = jnp.sum(parts_ref[...].reshape(-1, 2 * blocks, VMAX), axis=0)
    out_ref[...] = (total[:blocks] + total[blocks:]) / gap_ref[...]


def call(kernel, outs, in_memory, cost=None, out_memory=pltpu.VMEM, scratch=()):
    single = not isinstance(outs, list)
    shapes = [jax.ShapeDtypeStruct(*out) for out in ([outs] if single else outs)]
    specs = [pl.BlockSpec(memory_space=out_memory) for _ in shapes]
    return pl.pallas_call(
        kernel,
        out_shape=shapes[0] if single else shapes,
        in_specs=[pl.BlockSpec(memory_space=space) for space in in_memory],
        out_specs=specs[0] if single else specs,
        scratch_shapes=scratch,
        cost_estimate=cost,
        compiler_params=pltpu.CompilerParams(vmem_limit_bytes=VMEM_BYTES),
    )


def body(amplitudes, integrals, irrep_count, pair_energy, virt_energy):
    slabs = lax.axis_size("redist")
    owners = lax.axis_size("contract")
    chips = owners // CORES
    pairs, _, cells_all = amplitudes.shape
    _, cells, virt = integrals.shape
    parts = cells // VMAX
    blocks = virt // VMAX
    vmem, smem, hbm = pltpu.VMEM, pltpu.SMEM, pltpu.HBM
    f32, bf16 = jnp.float32, jnp.bfloat16
    axes = ("redist", "contract")
    same_chips = [
        [slab * owners + chip * CORES + core for slab in range(slabs) for core in range(CORES)]
        for chip in range(chips)
    ]
    same_core = [
        [slab * owners + chip * CORES + core for slab in range(slabs) for chip in range(chips)]
        for core in range(CORES)
    ]

    lines = pairs * parts
    grouped = call(
        regroup_kernel,
        ((slabs, lines, VMAX), f32),
        [hbm],
        out_memory=hbm,
        scratch=[
            pltpu.VMEM((CHUNKS, pairs, parts * slabs // CHUNKS, VMAX), f32),
            pltpu.VMEM((CHUNKS, slabs // CHUNKS, lines, VMAX), f32),
            pltpu.SemaphoreType.DMA((CHUNKS,)),
            pltpu.SemaphoreType.DMA((CHUNKS,)),
        ],
    )(amplitudes.reshape(pairs, cells_all // VMAX, VMAX))
    arrived = lax.all_to_all(
        grouped.reshape(slabs * CORES, -1, VMAX),
        axes,
        split_axis=0,
        concat_axis=0,
        axis_index_groups=same_chips,
        tiled=True,
    ).reshape(slabs, lines, VMAX)

    own = integrals.reshape(cells, virt)
    other = lax.ppermute(own, "contract", [(owner, owner ^ 1) for owner in range(owners)])
    high, low, gap = call(
        weights_kernel,
        [((CORES * cells, virt), bf16), ((CORES * cells, virt), bf16), ((blocks, VMAX), f32)],
        [smem, smem, vmem, vmem, vmem],
        cost=pl.CostEstimate(flops=10 * CORES * cells * virt, bytes_accessed=8 * CORES * cells * virt, transcendentals=0),
    )(irrep_count, pair_energy, own, other, virt_energy.reshape(blocks, VMAX))

    partial = call(ladder_kernel, ((slabs, chips * blocks, VMAX), f32), [vmem] * 3)(
        arrived, high, low
    )
    partial = lax.all_to_all(
        partial.reshape(-1, blocks, VMAX),
        axes,
        split_axis=0,
        concat_axis=0,
        axis_index_groups=same_core,
        tiled=True,
    )
    delta = call(finish_kernel, ((blocks, VMAX), f32), [vmem] * 2)(
        partial.reshape(-1, VMAX), gap
    )
    return delta.reshape(1, virt)


def solution(mesh):
    in_specs = (
        P("redist", "contract", None),
        P("contract", "redist", None),
        P(),
        P(("redist", "contract")),
        P(),
    )
    out_specs = P(("redist", "contract"), None)
    return jax.shard_map(body, mesh=mesh, in_specs=in_specs, out_specs=out_specs, check_vma=False)
```

time: 78.9 us -> 72.5 us (0.919)
  the two profiles are of different devices: /device:TPU:1 before, /device:TPU:8 now
where the time goes in v2:
time: 72.5 us; the launch traced here: 72.2 us
  blocking collectives  30.7 us (42%)
  starting transfers between devices  19.6 us (27%)
  waiting for transfers between devices  16.6 us (23%)
  Pallas kernels  3.63 us (5%)
  local copies, waits for them, and re-layouts  1.06 us (1%)
    all_to_all x1, blocking collectives, body(): lax.all_to_all(partial.reshape(-1, blocks, VMAX), axes, split_axis=0, con...  30.7 us
    all_to_all x1, starting transfers between devices, body(): lax.all_to_all(grouped.reshape(slabs * CORES, -1, VMAX), axes, split_axis...  17.5 us
    all_to_all x1, waiting for transfers between devices, body(): lax.all_to_all(grouped.reshape(slabs * CORES, -1, VMAX), axes, split_axis...  15.5 us
    ppermute x1, starting transfers between devices, body(): lax.ppermute(own, 'contract', [(owner, owner ^ 1) for owner in range(owne...  2.06 us
  transfers between devices with their start and end apart: 2, of which 2 were waited for; matrix products, arithmetic and copies ran while one was open for 0% of the time, Pallas kernels for 1%

profile of v2, /device:TPU:8, one launch (start us, length us, event | category | flops | bytes accessed | tf_op | source)
XLA Modules:
  0.0 72.2 jit_solution(17990206119752685663)
XLA Ops:
  0.0 0.0 copy-start.1
  0.0 1.0 %copy-done.1 = f32[8,1,16384]{2,1,0:T(1,128)S(1)} copy-done((f32[8,1,16384]{2,1,0:T(1,128)S(1)}, f32[8,1,16384]{2,1,0:T(1,128)}, u32[]{:S(2)}) %copy-start.1) | copy-done | bytes 524312
  1.0 1.1 %shard_map.55 = f32[64,16,128]{2,1,0:T(8,128)} custom-call(f32[8,128,128]{2,1,0:T(8,128)S(1)} %bitcast.13), custom_call_target="tpu_custom_call" | custom-call | tf_op jit(solution)/shard_map/pallas_call | solution.py:151
  2.2 0.0 copy-start
  2.2 17.5 %all-to-all-start = ((f32[128,8,128]{2,1,0:T(8,128)}), f32[128,8,128]{2,1,0:T(8,128)S(1)}, u32[]{:S(2)}, u32[]{:S(2)}) async-start(f32[128,8,128]{2,1,0:T(8,128)} %bitcast.1), calls=%async_computation | async-start | bytes 1048576 | tf_op jit(solution)/shard_map/all_to_all | solution.py:163
  19.7 0.0 copy-done
  19.7 0.0 copy-start.2
  19.7 2.1 %collective-permute-start = (f32[256,512]{1,0:T(8,128)S(1)}, f32[256,512]{1,0:T(8,128)S(1)}, u32[]{:S(2)}, u32[]{:S(2)}) collective-permute-start(f32[256,512]{1,0:T(8,128)S(1)} %bitcast.11), channel_id=1, source_target_pairs={{0,1},{1,0},{2,3},{3,2},{4,5},{5,4},{6,7},{7,6},{8,9},{9,8},{10,11... | collective-permute-start | bytes 1572872 | tf_op jit(solution)/shard_map/ppermute | solution.py:173
  22.4 0.0 copy-start.3
  22.4 1.1 %collective-permute-done.other_ref = f32[256,512]{1,0:T(8,128)S(1)} collective-permute-done((f32[256,512]{1,0:T(8,128)S(1)}, f32[256,512]{1,0:T(8,128)S(1)}, u32[]{:S(2)}, u32[]{:S(2)}) %collective-permute-start) | collective-permute-done | bytes 524320 | tf_op jit(solution)/shard_map/ppermute | solution.py:173
  23.5 0.0 copy-done.2
  23.5 0.0 copy-done.3
  23.5 0.9 %shard_map.56 = (bf16[512,512]{1,0:T(8,128)(2,1)S(1)}, bf16[512,512]{1,0:T(8,128)(2,1)S(1)}, f32[4,128]{1,0:T(4,128)S(1)}) custom-call(s32[8]{0:T(128)S(1)} %copy-done.3, f32[1]{0:T(128)S(6)} %copy.6.pair_energy_ref, f32[256,512]{1,0:T(8,128)S(1)} %bitcast.12, f32[256,512]{1,0:T(8,128)S(1)} %collective-permute-done.other_ref, f32[4,128]{1,0:T(4,128)S(1)} %bitcast.14), custom_call_target="tpu_custom_call" | custom-call | flops 2621440 | bytes 2097152 | tf_op jit(solution)/shard_map/pallas_call | solution.py:174
  24.4 15.5 %all-to-all-done = f32[128,8,128]{2,1,0:T(8,128)S(1)} async-done(((f32[128,8,128]{2,1,0:T(8,128)}), f32[128,8,128]{2,1,0:T(8,128)S(1)}, u32[]{:S(2)}, u32[]{:S(2)}) %all-to-all-start) | async-done | bytes 524320 | tf_op jit(solution)/shard_map/all_to_all | solution.py:163
  39.9 0.9 %shard_map.57 = f32[64,16,128]{2,1,0:T(8,128)S(1)} custom-call(f32[64,16,128]{2,1,0:T(8,128)S(1)} %bitcast.9, bf16[512,512]{1,0:T(8,128)(2,1)S(1)} %get-tuple-element.8.high_ref, bf16[512,512]{1,0:T(8,128)(2,1)S(1)} %get-tuple-element.9.low_ref), custom_call_target="tpu_custom_call" | custom-call | tf_op jit(solution)/shard_map/pallas_call | solution.py:181
  40.8 30.7 %all_to_all.10 = f32[256,4,128]{2,1,0:T(4,128)S(1)} all-to-all(f32[256,4,128]{2,1,0:T(4,128)S(1)} %bitcast.10), channel_id=1, replica_groups={{0,2,4,6,8,10,12,14,16,18,20,22,24,26,28,30,32,34,36,38,40,42,44,46,48,..., dimensions={0} | all-to-all | bytes 1048576 | tf_op jit(solution)/shard_map/all_to_all | solution.py:184
  71.5 0.7 shard_map.58
Async XLA Ops:
  0.0 1.0 %copy-start.1 = (f32[8,1,16384]{2,1,0:T(1,128)S(1)}, f32[8,1,16384]{2,1,0:T(1,128)}, u32[]{:S(2)}) copy-start(f32[8,1,16384]{2,1,0:T(1,128)} %param.5) | copy-start | bytes 1572868
  2.2 17.5 %copy-start = (f32[1,256,512]{2,1,0:T(8,128)S(1)}, f32[1,256,512]{2,1,0:T(8,128)}, u32[]{:S(2)}) copy-start(f32[1,256,512]{2,1,0:T(8,128)} %param.6) | copy-start | bytes 1572868
  2.2 37.7 %all-to-all-start = ((f32[128,8,128]{2,1,0:T(8,128)}), f32[128,8,128]{2,1,0:T(8,128)S(1)}, u32[]{:S(2)}, u32[]{:S(2)}) async-start(f32[128,8,128]{2,1,0:T(8,128)} %bitcast.1), calls=%async_computation | async-start | bytes 1048576 | tf_op jit(solution)/shard_map/all_to_all | solution.py:163
  19.7 3.8 %copy-start.2 = (f32[512]{0:T(512)S(1)}, f32[512]{0:T(512)}, u32[]{:S(2)}) copy-start(f32[512]{0:T(512)} %param.9) | copy-start | bytes 6148
  19.7 3.8 %collective-permute-start = (f32[256,512]{1,0:T(8,128)S(1)}, f32[256,512]{1,0:T(8,128)S(1)}, u32[]{:S(2)}, u32[]{:S(2)}) collective-permute-start(f32[256,512]{1,0:T(8,128)S(1)} %bitcast.11), channel_id=1, source_target_pairs={{0,1},{1,0},{2,3},{3,2},{4,5},{5,4},{6,7},{7,6},{8,9},{9,8},{10,11... | collective-permute-start | bytes 1572872 | tf_op jit(solution)/shard_map/ppermute | solution.py:173
  22.4 1.1 %copy-start.3 = (s32[8]{0:T(128)S(1)}, s32[8]{0:T(128)}, u32[]{:S(2)}) copy-start(s32[8]{0:T(128)} %count_ref.1) | copy-start | bytes 100

commit v3 on v2

v3 whole, which is shorter than its diff:
```python
import jax
import jax.numpy as jnp
from jax import lax
from jax.experimental import pallas as pl
from jax.experimental.pallas import tpu as pltpu
from jax.sharding import PartitionSpec as P

VMAX = 128
GAMMA = 3
CORES = 2
SLABS = 2
CHUNKS = 4
VMEM_BYTES = 48 * 1024 * 1024


def regroup_kernel(cells_ref, out_ref, ready, sems):
    pairs, all_lines, _ = cells_ref.shape
    places, lines, _ = out_ref.shape
    parts = lines // pairs
    chunks = sems.shape[0]
    places_each, lines_each = places // chunks, all_lines // chunks
    copies = []
    for chunk in range(chunks):
        for pair in range(pairs):
            line = (pair % CORES) * (lines // CORES) + (pair // CORES) * parts
            for part in range(parts):
                ready[chunk, :, line + part, :] = cells_ref[
                    pair, pl.ds(chunk * lines_each + part, places_each, stride=parts), :
                ]
        copies.append(
            pltpu.make_async_copy(
                ready.at[chunk],
                out_ref.at[pl.ds(chunk * places_each, places_each)],
                sems.at[chunk],
            )
        )
        copies[chunk].start()
    for copy in copies:
        copy.wait()


def split_bf16(value):
    high = value.astype(jnp.bfloat16)
    return high, (value - high.astype(jnp.float32)).astype(jnp.bfloat16)


def weights_kernel(count_ref, pair_energy_ref, virt_energy_ref, *refs):
    held_refs, (high_ref, low_ref, gap_ref) = refs[: CORES * SLABS], refs[CORES * SLABS :]
    cells, virt = held_refs[0].shape
    parts = cells // VMAX
    cell = lax.broadcasted_iota(jnp.int32, (cells, virt), 0)
    for turn, held_ref in enumerate(held_refs):
        irrep = jnp.bitwise_xor(lax.axis_index("contract"), turn // SLABS)
        slab = jnp.bitwise_xor(lax.axis_index("redist"), turn % SLABS)
        row, col = slab * parts + cell // VMAX, cell % VMAX
        live = (row < count_ref[irrep]) & (col < count_ref[jnp.bitwise_xor(irrep, GAMMA)])
        high, low = split_bf16(jnp.where(live, 0.5 * held_ref[...], 0.0))
        place = pl.multiple_of((irrep % CORES * SLABS + slab % SLABS) * cells, cells)
        high_ref[pl.ds(place, cells), :] = high
        low_ref[pl.ds(place, cells), :] = low
    gap_ref[...] = virt_energy_ref[...] - pair_energy_ref[0]


def ladder_kernel(rows_ref, high_ref, low_ref, out_ref):
    places, lines, _ = rows_ref.shape
    depth, virt = high_ref.shape
    blocks = virt // VMAX
    turns = out_ref.shape[1] // blocks
    parts = depth // VMAX // CORES
    rows = jnp.concatenate(
        [
            jnp.concatenate(
                [
                    rows_ref[:, (source * turns + turn) * parts + part, :]
                    for source in range(CORES)
                    for part in range(parts)
                ],
                axis=1,
            )
            for turn in range(turns)
        ],
        axis=0,
    )
    rows_high, rows_low = split_bf16(rows)
    high, low = high_ref[...], low_ref[...]
    total = jnp.dot(rows_high, low, preferred_element_type=jnp.float32)
    total = total + jnp.dot(rows_low, high, preferred_element_type=jnp.float32)
    total = total + jnp.dot(rows_high, high, preferred_element_type=jnp.float32)
    for turn in range(turns):
        for block in range(blocks):
            out_ref[:, turn * blocks + block, :] = total[
                turn * places : (turn + 1) * places, block * VMAX : (block + 1) * VMAX
            ]


def finish_kernel(parts_ref, gap_ref, out_ref):
    blocks = out_ref.shape[0]
    total = jnp.sum(parts_ref[...].reshape(-1, 2 * blocks, VMAX), axis=0)
    out_ref[...] = (total[:blocks] + total[blocks:]) / gap_ref[...]


def call(kernel, outs, in_memory, cost=None, out_memory=pltpu.VMEM, scratch=()):
    single = not isinstance(outs, list)
    shapes = [jax.ShapeDtypeStruct(*out) for out in ([outs] if single else outs)]
    specs = [pl.BlockSpec(memory_space=out_memory) for _ in shapes]
    return pl.pallas_call(
        kernel,
        out_shape=shapes[0] if single else shapes,
        in_specs=[pl.BlockSpec(memory_space=space) for space in in_memory],
        out_specs=specs[0] if single else specs,
        scratch_shapes=scratch,
        cost_estimate=cost,
        compiler_params=pltpu.CompilerParams(vmem_limit_bytes=VMEM_BYTES),
    )


def body(amplitudes, integrals, irrep_count, pair_energy, virt_energy):
    slabs = lax.axis_size("redist")
    owners = lax.axis_size("contract")
    pairs, _, cells_all = amplitudes.shape
    _, cells, virt = integrals.shape
    blocks = virt // VMAX
    places, chips = slabs // SLABS, owners // CORES
    vmem, smem = pltpu.VMEM, pltpu.SMEM
    f32, bf16 = jnp.float32, jnp.bfloat16

    def device(place, side, chip, core):
        slab = place * SLABS + (side ^ (place // 2 % 2))
        return slab * owners + chip * CORES + core

    same_chip = [
        [device(place, side, chip, core) for place in range(places) for core in range(CORES)]
        for side in range(SLABS)
        for chip in range(chips)
    ]
    same_core = [
        [device(place, side, chip, core) for place in range(places) for chip in range(chips)]
        for side in range(SLABS)
        for core in range(CORES)
    ]

    def exchange(blocks_out, groups):
        return lax.all_to_all(
            blocks_out,
            ("redist", "contract"),
            split_axis=0,
            concat_axis=0,
            axis_index_groups=groups,
            tiled=True,
        )

    def swap(block, axis):
        count = lax.axis_size(axis)
        return lax.ppermute(block, axis, [(index, index ^ 1) for index in range(count)])

    own = integrals.reshape(cells, virt)
    held = [own, swap(own, "redist")]
    held = held + [swap(block, "contract") for block in held]

    all_lines = cells_all // VMAX
    lines = pairs * all_lines // places
    grouped = call(
        regroup_kernel,
        ((places, lines, VMAX), f32),
        [vmem],
        out_memory=pltpu.HBM,
        scratch=[
            pltpu.VMEM((CHUNKS, places // CHUNKS, lines, VMAX), f32),
            pltpu.SemaphoreType.DMA((CHUNKS,)),
        ],
    )(amplitudes.reshape(pairs, all_lines, VMAX))
    arrived = exchange(grouped.reshape(places * CORES, lines // CORES, VMAX), same_chip)

    depth = CORES * SLABS * cells
    high, low, gap = call(
        weights_kernel,
        [((depth, virt), bf16), ((depth, virt), bf16), ((blocks, VMAX), f32)],
        [smem, smem, vmem] + [vmem] * len(held),
        cost=pl.CostEstimate(
            flops=10 * depth * virt, bytes_accessed=8 * depth * virt, transcendentals=0
        ),
    )(irrep_count, pair_energy, virt_energy.reshape(blocks, VMAX), *held)

    partial = call(ladder_kernel, ((places, chips * blocks, VMAX), f32), [vmem] * 3)(
        arrived.reshape(places, lines, VMAX), high, low
    )
    partial = exchange(partial.reshape(places * chips, blocks, VMAX), same_core)
    delta = call(finish_kernel, ((blocks, VMAX), f32), [vmem] * 2)(
        partial.reshape(-1, VMAX), gap
    )
    return delta.reshape(1, virt)


def solution(mesh):
    in_specs = (
        P("redist", "contract", None),
        P("contract", "redist", None),
        P(),
        P(("redist", "contract")),
        P(),
    )
    out_specs = P(("redist", "contract"), None)
    return jax.shard_map(body, mesh=mesh, in_specs=in_specs, out_specs=out_specs, check_vma=False)
```

time: 72.5 us -> 67.7 us (0.934)
  waiting for transfers between devices: 16.6 us -> 10.8 us
  blocking collectives: 30.7 us -> 26 us
  starting transfers between devices: 19.6 us -> 22.6 us
  local copies, waits for them, and re-layouts: 1.06 us -> 3.44 us
    ppermute x1 -> x3, starting transfers between devices: 2.06 us -> 12 us  [swap(): lax.ppermute(block, axis, [(index, index ^ 1) for index in range(count)])]
    all_to_all x1, starting transfers between devices: 17.5 us -> 10.6 us  [exchange(): lax.all_to_all(blocks_out, ('redist', 'contract'), split_axis=0, concat_a...]
    all_to_all x1, waiting for transfers between devices: 15.5 us -> 10.7 us  [exchange(): lax.all_to_all(blocks_out, ('redist', 'contract'), split_axis=0, concat_a...]
    all_to_all x1, blocking collectives: 30.7 us -> 26 us  [exchange(): lax.all_to_all(blocks_out, ('redist', 'contract'), split_axis=0, concat_a...]
    unnamed x8 -> x12, local copies, waits for them, and re-layouts: 1.06 us -> 3.44 us
    ppermute x1 -> x3, waiting for transfers between devices: 1.08 us -> 0.06 us  [swap(): lax.ppermute(block, axis, [(index, index ^ 1) for index in range(count)])]
  transfers between devices with their start and end apart: 2 -> 4, of which waited for: 2 -> 2; matrix products, arithmetic and copies ran while one was open for 0% -> 0% of each run, Pallas kernels for 1% -> 3%
where the time goes in v3:
time: 67.7 us; the launch traced here: 67.3 us
  blocking collectives  26 us (38%)
  starting transfers between devices  22.6 us (33%)
  waiting for transfers between devices  10.8 us (16%)
  Pallas kernels  3.66 us (5%)
  local copies, waits for them, and re-layouts  3.44 us (5%)
  between operations  0.77 us (1%)
    all_to_all x1, blocking collectives, exchange(): lax.all_to_all(blocks_out, ('redist', 'contract'), split_axis=0, concat_a...  26 us
    ppermute x3, starting transfers between devices, swap(): lax.ppermute(block, axis, [(index, index ^ 1) for index in range(count)])  12 us
    all_to_all x1, waiting for transfers between devices, exchange(): lax.all_to_all(blocks_out, ('redist', 'contract'), split_axis=0, concat_a...  10.7 us
    all_to_all x1, starting transfers between devices, exchange(): lax.all_to_all(blocks_out, ('redist', 'contract'), split_axis=0, concat_a...  10.6 us
    unnamed x12, local copies, waits for them, and re-layouts  3.44 us
  transfers between devices with their start and end apart: 4, of which 2 were waited for; matrix products, arithmetic and copies ran while one was open for 0% of the time, Pallas kernels for 3%

profile of v3, /device:TPU:8, one launch (start us, length us, event | category | flops | bytes accessed | tf_op | source)
XLA Modules:
  0.0 67.3 jit_solution(1273737948422588452)
XLA Ops:
  0.0 7.7 %collective-permute-start = (f32[256,512]{1,0:T(8,128)}, f32[256,512]{1,0:T(8,128)S(1)}, u32[]{:S(2)}, u32[]{:S(2)}) collective-permute-start(f32[256,512]{1,0:T(8,128)} %bitcast.11), channel_id=1, source_target_pairs={{0,8},{8,0},{16,24},{24,16},{32,40},{40,32},{48,56},{56,48},{64,72... | collective-permute-start | bytes 1572872 | tf_op jit(solution)/shard_map/ppermute | solution.py:154
  7.7 0.0 copy-start.3
  7.7 1.0 %copy-done.3 = f32[8,1,16384]{2,1,0:T(1,128)S(1)} copy-done((f32[8,1,16384]{2,1,0:T(1,128)S(1)}, f32[8,1,16384]{2,1,0:T(1,128)}, u32[]{:S(2)}) %copy-start.3) | copy-done | bytes 524312
  8.8 1.0 %shard_map.55 = f32[32,32,128]{2,1,0:T(8,128)} custom-call(f32[8,128,128]{2,1,0:T(8,128)S(1)} %bitcast.14), custom_call_target="tpu_custom_call" | custom-call | tf_op jit(solution)/shard_map/pallas_call | solution.py:162
  9.8 0.0 copy-start
  9.8 10.6 %all-to-all-start = ((f32[64,16,128]{2,1,0:T(8,128)}), f32[64,16,128]{2,1,0:T(8,128)S(1)}, u32[]{:S(2)}, u32[]{:S(2)}) async-start(f32[64,16,128]{2,1,0:T(8,128)} %bitcast.1), calls=%async_computation | async-start | bytes 1048576 | tf_op jit(solution)/shard_map/all_to_all | solution.py:143
  20.3 0.0 copy-done
  20.4 0.0 copy-start.4
  20.4 2.0 %collective-permute-start.1 = (f32[256,512]{1,0:T(8,128)S(1)}, f32[256,512]{1,0:T(8,128)S(1)}, u32[]{:S(2)}, u32[]{:S(2)}) collective-permute-start(f32[256,512]{1,0:T(8,128)S(1)} %bitcast.12), channel_id=1, source_target_pairs={{0,1},{1,0},{2,3},{3,2},{4,5},{5,4},{6,7},{7,6},{8,9},{9,8},{10,11... | collective-permute-start | bytes 1572872 | tf_op jit(solution)/shard_map/ppermute | solution.py:154
  22.3 0.0 collective-permute-done.refs_1_
  22.3 2.4 %collective-permute-start.2 = (f32[256,512]{1,0:T(8,128)S(1)}, f32[256,512]{1,0:T(8,128)S(1)}, u32[]{:S(2)}, u32[]{:S(2)}) collective-permute-start(f32[256,512]{1,0:T(8,128)S(1)} %collective-permute-done.refs_1_), channel_id=1, source_target_pairs={{0,1},{1,0},{2,3},{3,2},{4,5},{5,4},{6,7},{7,6},{8,9},{9,8},{10,11... | collective-permute-start | bytes 1572872 | tf_op jit(solution)/shard_map/ppermute | solution.py:154
  24.7 0.0 copy-start.1
  24.7 0.8 %copy-done.1 = f32[256,512]{1,0:T(8,128)} copy-done((f32[256,512]{1,0:T(8,128)}, f32[256,512]{1,0:T(8,128)S(1)}, u32[]{:S(2)}) %copy-start.1) | copy-done | bytes 524312
  26.2 0.0 copy-start.5
  26.2 0.0 collective-permute-done.1.refs_2_
  26.2 0.1 collective-permute-done.2.refs_3_
  26.2 0.0 copy-done.4
  26.2 0.6 copy-done.5
  26.8 1.0 %copy-done.2 = f32[256,512]{1,0:T(8,128)S(1)} copy-done((f32[256,512]{1,0:T(8,128)S(1)}, f32[256,512]{1,0:T(8,128)}, u32[]{:S(2)}) %copy-start.2) | copy-done | bytes 524312
  27.9 1.1 %shard_map.56 = (bf16[1024,512]{1,0:T(8,128)(2,1)S(1)}, bf16[1024,512]{1,0:T(8,128)(2,1)S(1)}, f32[4,128]{1,0:T(4,128)S(1)}) custom-call(s32[8]{0:T(128)S(1)} %copy-done.5, f32[1]{0:T(128)S(6)} %copy.6.pair_energy_ref, f32[4,128]{1,0:T(4,128)S(1)} %bitcast.15, f32[256,512]{1,0:T(8,128)S(1)} %bitcast.13, f32[256,512]{1,0:T(8,128)S(1)} %copy-done.2, ...), custom_call_target="tpu_custom_call" | custom-call | flops 5242880 | bytes 4194304 | tf_op jit(solution)/shard_map/pallas_call | solution.py:175
  29.0 10.7 %all-to-all-done = f32[64,16,128]{2,1,0:T(8,128)S(1)} async-done(((f32[64,16,128]{2,1,0:T(8,128)}), f32[64,16,128]{2,1,0:T(8,128)S(1)}, u32[]{:S(2)}, u32[]{:S(2)}) %all-to-all-start) | async-done | bytes 524320 | tf_op jit(solution)/shard_map/all_to_all | solution.py:143
  39.7 0.9 %shard_map.57 = f32[32,16,128]{2,1,0:T(8,128)S(1)} custom-call(f32[32,32,128]{2,1,0:T(8,128)S(1)} %bitcast.8, bf16[1024,512]{1,0:T(8,128)(2,1)S(1)} %get-tuple-element.8.high_ref, bf16[1024,512]{1,0:T(8,128)(2,1)S(1)} %get-tuple-element.9.low_ref), custom_call_target="tpu_custom_call" | custom-call | tf_op jit(solution)/shard_map/pallas_call | solution.py:184
  40.6 26.0 %all_to_all.10 = f32[128,4,128]{2,1,0:T(4,128)S(1)} all-to-all(f32[128,4,128]{2,1,0:T(4,128)S(1)} %bitcast.10), channel_id=1, replica_groups={{0,2,4,6,16,18,20,22,40,42,44,46,56,58,60,62,64,66,68,70,80,82,84,86,10..., dimensions={0} | all-to-all | bytes 524288 | tf_op jit(solution)/shard_map/all_to_all | solution.py:143
  66.7 0.6 shard_map.58
  (1 shorter events, 0.0 us)
Async XLA Ops:
  0.0 22.3 %collective-permute-start = (f32[256,512]{1,0:T(8,128)}, f32[256,512]{1,0:T(8,128)S(1)}, u32[]{:S(2)}, u32[]{:S(2)}) collective-permute-start(f32[256,512]{1,0:T(8,128)} %bitcast.11), channel_id=1, source_target_pairs={{0,8},{8,0},{16,24},{24,16},{32,40},{40,32},{48,56},{56,48},{64,72... | collective-permute-start | bytes 1572872 | tf_op jit(solution)/shard_map/ppermute | solution.py:154
  7.7 1.0 %copy-start.3 = (f32[8,1,16384]{2,1,0:T(1,128)S(1)}, f32[8,1,16384]{2,1,0:T(1,128)}, u32[]{:S(2)}) copy-start(f32[8,1,16384]{2,1,0:T(1,128)} %param.5) | copy-start | bytes 1572868
  9.8 10.6 %copy-start = (f32[1,256,512]{2,1,0:T(8,128)S(1)}, f32[1,256,512]{2,1,0:T(8,128)}, u32[]{:S(2)}) copy-start(f32[1,256,512]{2,1,0:T(8,128)} %param.6) | copy-start | bytes 1572868
  9.8 30.0 %all-to-all-start = ((f32[64,16,128]{2,1,0:T(8,128)}), f32[64,16,128]{2,1,0:T(8,128)S(1)}, u32[]{:S(2)}, u32[]{:S(2)}) async-start(f32[64,16,128]{2,1,0:T(8,128)} %bitcast.1), calls=%async_computation | async-start | bytes 1048576 | tf_op jit(solution)/shard_map/all_to_all | solution.py:143
  20.4 5.9 %copy-start.4 = (f32[512]{0:T(512)S(1)}, f32[512]{0:T(512)}, u32[]{:S(2)}) copy-start(f32[512]{0:T(512)} %param.9) | copy-start | bytes 6148
  20.4 5.8 %collective-permute-start.1 = (f32[256,512]{1,0:T(8,128)S(1)}, f32[256,512]{1,0:T(8,128)S(1)}, u32[]{:S(2)}, u32[]{:S(2)}) collective-permute-start(f32[256,512]{1,0:T(8,128)S(1)} %bitcast.12), channel_id=1, source_target_pairs={{0,1},{1,0},{2,3},{3,2},{4,5},{5,4},{6,7},{7,6},{8,9},{9,8},{10,11... | collective-permute-start | bytes 1572872 | tf_op jit(solution)/shard_map/ppermute | solution.py:154
  22.3 3.9 %collective-permute-start.2 = (f32[256,512]{1,0:T(8,128)S(1)}, f32[256,512]{1,0:T(8,128)S(1)}, u32[]{:S(2)}, u32[]{:S(2)}) collective-permute-start(f32[256,512]{1,0:T(8,128)S(1)} %collective-permute-done.refs_1_), channel_id=1, source_target_pairs={{0,1},{1,0},{2,3},{3,2},{4,5},{5,4},{6,7},{7,6},{8,9},{9,8},{10,11... | collective-permute-start | bytes 1572872 | tf_op jit(solution)/shard_map/ppermute | solution.py:154
  24.7 0.8 %copy-start.1 = (f32[256,512]{1,0:T(8,128)}, f32[256,512]{1,0:T(8,128)S(1)}, u32[]{:S(2)}) copy-start(f32[256,512]{1,0:T(8,128)S(1)} %collective-permute-done.refs_1_) | copy-start | bytes 1572868
  26.2 0.7 copy-start.5
  26.8 1.0 %copy-start.2 = (f32[256,512]{1,0:T(8,128)S(1)}, f32[256,512]{1,0:T(8,128)}, u32[]{:S(2)}) copy-start(f32[256,512]{1,0:T(8,128)} %copy-done.1) | copy-start | bytes 1572868

commit v4 on v3

--- a/solution.py
+++ b/solution.py
@@ -1,3 +1,5 @@
+import functools
+
 import jax
 import jax.numpy as jnp
 from jax import lax
@@ -10,10 +12,17 @@
 CORES = 2
 SLABS = 2
 CHUNKS = 4
+RING = 8
 VMEM_BYTES = 48 * 1024 * 1024
 
 
-def regroup_kernel(cells_ref, out_ref, ready, sems):
+def first_swapped(count, first):
+    order = list(range(count))
+    order[0], order[first] = first, 0
+    return order
+
+
+def regroup_kernel(place_order, cells_ref, out_ref, ready, sems):
     pairs, all_lines, _ = cells_ref.shape
     places, lines, _ = out_ref.shape
     parts = lines // pairs
@@ -27,6 +36,12 @@
                 ready[chunk, :, line + part, :] = cells_ref[
                     pair, pl.ds(chunk * lines_each + part, places_each, stride=parts), :
                 ]
+            for index in range(places_each):
+                place = place_order[chunk * places_each + index]
+                if place != chunk * places_each + index:
+                    ready[chunk, index, line : line + parts, :] = cells_ref[
+                        pair, place * parts : (place + 1) * parts, :
+                    ]
         copies.append(
             pltpu.make_async_copy(
                 ready.at[chunk],
@@ -61,7 +76,7 @@
     gap_ref[...] = virt_energy_ref[...] - pair_energy_ref[0]
 
 
-def ladder_kernel(rows_ref, high_ref, low_ref, out_ref):
+def ladder_kernel(chip_order, rows_ref, high_ref, low_ref, out_ref):
     places, lines, _ = rows_ref.shape
     depth, virt = high_ref.shape
     blocks = virt // VMAX
@@ -86,9 +101,9 @@
     total = jnp.dot(rows_high, low, preferred_element_type=jnp.float32)
     total = total + jnp.dot(rows_low, high, preferred_element_type=jnp.float32)
     total = total + jnp.dot(rows_high, high, preferred_element_type=jnp.float32)
-    for turn in range(turns):
+    for index, turn in enumerate(chip_order):
         for block in range(blocks):
-            out_ref[:, turn * blocks + block, :] = total[
+            out_ref[:, index * blocks + block, :] = total[
                 turn * places : (turn + 1) * places, block * VMAX : (block + 1) * VMAX
             ]
 
@@ -128,13 +143,16 @@
         slab = place * SLABS + (side ^ (place // 2 % 2))
         return slab * owners + chip * CORES + core
 
+    columns = RING // SLABS
+    place_order = first_swapped(places, places // 2 + columns // 2)
+    chip_order = first_swapped(chips, chips // 2)
     same_chip = [
-        [device(place, side, chip, core) for place in range(places) for core in range(CORES)]
+        [device(place, side, chip, core) for place in place_order for core in range(CORES)]
         for side in range(SLABS)
         for chip in range(chips)
     ]
     same_core = [
-        [device(place, side, chip, core) for place in range(places) for chip in range(chips)]
+        [device(place, side, chip, core) for place in place_order for chip in chip_order]
         for side in range(SLABS)
         for core in range(CORES)
     ]
@@ -160,7 +178,7 @@
     all_lines = cells_all // VMAX
     lines = pairs * all_lines // places
     grouped = call(
-        regroup_kernel,
+        functools.partial(regroup_kernel, place_order),
         ((places, lines, VMAX), f32),
         [vmem],
         out_memory=pltpu.HBM,
@@ -181,9 +199,11 @@
         ),
     )(irrep_count, pair_energy, virt_energy.reshape(blocks, VMAX), *held)
 
-    partial = call(ladder_kernel, ((places, chips * blocks, VMAX), f32), [vmem] * 3)(
-        arrived.reshape(places, lines, VMAX), high, low
-    )
+    partial = call(
+        functools.partial(ladder_kernel, chip_order),
+        ((places, chips * blocks, VMAX), f32),
+        [vmem] * 3,
+    )(arrived.reshape(places, lines, VMAX), high, low)
     partial = exchange(partial.reshape(places * chips, blocks, VMAX), same_core)
     delta = call(finish_kernel, ((blocks, VMAX), f32), [vmem] * 2)(
         partial.reshape(-1, VMAX), gap

time: 67.7 us -> 62 us (0.916)
  the two profiles are of different devices: /device:TPU:8 before, /device:TPU:1 now
where the time goes in v4:
time: 62 us; the launch traced here: 61.5 us
  starting transfers between devices  28.4 us (46%)
  blocking collectives  21.3 us (34%)
  waiting for transfers between devices  4.21 us (7%)
  Pallas kernels  3.69 us (6%)
  local copies, waits for them, and re-layouts  3.22 us (5%)
  between operations  0.77 us (1%)
    all_to_all x1, blocking collectives, exchange(): lax.all_to_all(blocks_out, ('redist', 'contract'), split_axis=0, concat_a...  21.3 us
    all_to_all x1, starting transfers between devices, exchange(): lax.all_to_all(blocks_out, ('redist', 'contract'), split_axis=0, concat_a...  20 us
    ppermute x3, starting transfers between devices, swap(): lax.ppermute(block, axis, [(index, index ^ 1) for index in range(count)])  8.35 us
    all_to_all x1, waiting for transfers between devices, exchange(): lax.all_to_all(blocks_out, ('redist', 'contract'), split_axis=0, concat_a...  3.92 us
    unnamed x12, local copies, waits for them, and re-layouts  3.22 us
  transfers between devices with their start and end apart: 4, of which 2 were waited for; matrix products, arithmetic and copies ran while one was open for 0% of the time, Pallas kernels for 3%

profile of v4, /device:TPU:1, one launch (start us, length us, event | category | flops | bytes accessed | tf_op | source)
XLA Modules:
  0.0 61.5 jit_solution(18148070479598921337)
XLA Ops:
  0.0 4.0 %collective-permute-start = (f32[256,512]{1,0:T(8,128)}, f32[256,512]{1,0:T(8,128)S(1)}, u32[]{:S(2)}, u32[]{:S(2)}) collective-permute-start(f32[256,512]{1,0:T(8,128)} %bitcast.11), channel_id=1, source_target_pairs={{0,8},{8,0},{16,24},{24,16},{32,40},{40,32},{48,56},{56,48},{64,72... | collective-permute-start | bytes 1572872 | tf_op jit(solution)/shard_map/ppermute | solution.py:172
  4.0 0.0 copy-start.3
  4.0 1.0 %copy-done.3 = f32[8,1,16384]{2,1,0:T(1,128)S(1)} copy-done((f32[8,1,16384]{2,1,0:T(1,128)S(1)}, f32[8,1,16384]{2,1,0:T(1,128)}, u32[]{:S(2)}) %copy-start.3) | copy-done | bytes 524312
  5.1 1.0 %shard_map.55 = f32[32,32,128]{2,1,0:T(8,128)} custom-call(f32[8,128,128]{2,1,0:T(8,128)S(1)} %bitcast.14), custom_call_target="tpu_custom_call" | custom-call | tf_op jit(solution)/shard_map/pallas_call | solution.py:180
  6.1 0.0 copy-start
  6.1 20.0 %all-to-all-start = ((f32[64,16,128]{2,1,0:T(8,128)}), f32[64,16,128]{2,1,0:T(8,128)S(1)}, u32[]{:S(2)}, u32[]{:S(2)}) async-start(f32[64,16,128]{2,1,0:T(8,128)} %bitcast.1), calls=%async_computation | async-start | bytes 1048576 | tf_op jit(solution)/shard_map/all_to_all | solution.py:161
  26.1 0.0 copy-done
  26.1 0.0 copy-start.4
  26.1 2.3 %collective-permute-start.1 = (f32[256,512]{1,0:T(8,128)S(1)}, f32[256,512]{1,0:T(8,128)S(1)}, u32[]{:S(2)}, u32[]{:S(2)}) collective-permute-start(f32[256,512]{1,0:T(8,128)S(1)} %bitcast.12), channel_id=1, source_target_pairs={{0,1},{1,0},{2,3},{3,2},{4,5},{5,4},{6,7},{7,6},{8,9},{9,8},{10,11... | collective-permute-start | bytes 1572872 | tf_op jit(solution)/shard_map/ppermute | solution.py:172
  28.4 0.0 collective-permute-done.refs_1_
  28.4 2.1 %collective-permute-start.2 = (f32[256,512]{1,0:T(8,128)S(1)}, f32[256,512]{1,0:T(8,128)S(1)}, u32[]{:S(2)}, u32[]{:S(2)}) collective-permute-start(f32[256,512]{1,0:T(8,128)S(1)} %collective-permute-done.refs_1_), channel_id=1, source_target_pairs={{0,1},{1,0},{2,3},{3,2},{4,5},{5,4},{6,7},{7,6},{8,9},{9,8},{10,11... | collective-permute-start | bytes 1572872 | tf_op jit(solution)/shard_map/ppermute | solution.py:172
  30.5 0.0 copy-start.1
  30.5 0.8 %copy-done.1 = f32[256,512]{1,0:T(8,128)} copy-done((f32[256,512]{1,0:T(8,128)}, f32[256,512]{1,0:T(8,128)S(1)}, u32[]{:S(2)}) %copy-start.1) | copy-done | bytes 524312
  31.9 0.0 copy-start.5
  31.9 0.0 collective-permute-done.1.refs_2_
  32.0 0.3 collective-permute-done.2.refs_3_
  32.2 0.0 copy-done.4
  32.2 0.3 copy-done.5
  32.6 1.0 %copy-done.2 = f32[256,512]{1,0:T(8,128)S(1)} copy-done((f32[256,512]{1,0:T(8,128)S(1)}, f32[256,512]{1,0:T(8,128)}, u32[]{:S(2)}) %copy-start.2) | copy-done | bytes 524312
  33.6 1.1 %shard_map.56 = (bf16[1024,512]{1,0:T(8,128)(2,1)S(1)}, bf16[1024,512]{1,0:T(8,128)(2,1)S(1)}, f32[4,128]{1,0:T(4,128)S(1)}) custom-call(s32[8]{0:T(128)S(1)} %copy-done.5, f32[1]{0:T(128)S(6)} %copy.6.pair_energy_ref, f32[4,128]{1,0:T(4,128)S(1)} %bitcast.15, f32[256,512]{1,0:T(8,128)S(1)} %bitcast.13, f32[256,512]{1,0:T(8,128)S(1)} %copy-done.2, ...), custom_call_target="tpu_custom_call" | custom-call | flops 5242880 | bytes 4194304 | tf_op jit(solution)/shard_map/pallas_call | solution.py:193
  34.8 3.9 %all-to-all-done = f32[64,16,128]{2,1,0:T(8,128)S(1)} async-done(((f32[64,16,128]{2,1,0:T(8,128)}), f32[64,16,128]{2,1,0:T(8,128)S(1)}, u32[]{:S(2)}, u32[]{:S(2)}) %all-to-all-start) | async-done | bytes 524320 | tf_op jit(solution)/shard_map/all_to_all | solution.py:161
  38.7 0.9 %shard_map.57 = f32[32,16,128]{2,1,0:T(8,128)S(1)} custom-call(f32[32,32,128]{2,1,0:T(8,128)S(1)} %bitcast.8, bf16[1024,512]{1,0:T(8,128)(2,1)S(1)} %get-tuple-element.8.high_ref, bf16[1024,512]{1,0:T(8,128)(2,1)S(1)} %get-tuple-element.9.low_ref), custom_call_target="tpu_custom_call" | custom-call | tf_op jit(solution)/shard_map/pallas_call | solution.py:202
  39.6 21.3 %all_to_all.10 = f32[128,4,128]{2,1,0:T(4,128)S(1)} all-to-all(f32[128,4,128]{2,1,0:T(4,128)S(1)} %bitcast.10), channel_id=1, replica_groups={{300,298,296,302,20,18,16,22,44,42,40,46,60,58,56,62,68,66,64,70,84,82,..., dimensions={0} | all-to-all | bytes 524288 | tf_op jit(solution)/shard_map/all_to_all | solution.py:161
  60.9 0.6 %shard_map.58 = f32[4,128]{1,0:T(4,128)} custom-call(f32[512,128]{1,0:T(8,128)S(1)} %bitcast.9, f32[4,128]{1,0:T(4,128)S(1)} %get-tuple-element.10.gap_ref), custom_call_target="tpu_custom_call" | custom-call | tf_op jit(solution)/shard_map/pallas_call | solution.py:208
  (1 shorter events, 0.0 us)
Async XLA Ops:
  0.0 28.4 %collective-permute-start = (f32[256,512]{1,0:T(8,128)}, f32[256,512]{1,0:T(8,128)S(1)}, u32[]{:S(2)}, u32[]{:S(2)}) collective-permute-start(f32[256,512]{1,0:T(8,128)} %bitcast.11), channel_id=1, source_target_pairs={{0,8},{8,0},{16,24},{24,16},{32,40},{40,32},{48,56},{56,48},{64,72... | collective-permute-start | bytes 1572872 | tf_op jit(solution)/shard_map/ppermute | solution.py:172
  4.0 1.0 %copy-start.3 = (f32[8,1,16384]{2,1,0:T(1,128)S(1)}, f32[8,1,16384]{2,1,0:T(1,128)}, u32[]{:S(2)}) copy-start(f32[8,1,16384]{2,1,0:T(1,128)} %param.5) | copy-start | bytes 1572868
  6.1 20.1 %copy-start = (f32[1,256,512]{2,1,0:T(8,128)S(1)}, f32[1,256,512]{2,1,0:T(8,128)}, u32[]{:S(2)}) copy-start(f32[1,256,512]{2,1,0:T(8,128)} %param.6) | copy-start | bytes 1572868
  6.1 32.6 %all-to-all-start = ((f32[64,16,128]{2,1,0:T(8,128)}), f32[64,16,128]{2,1,0:T(8,128)S(1)}, u32[]{:S(2)}, u32[]{:S(2)}) async-start(f32[64,16,128]{2,1,0:T(8,128)} %bitcast.1), calls=%async_computation | async-start | bytes 1048576 | tf_op jit(solution)/shard_map/all_to_all | solution.py:161
  26.1 6.1 %copy-start.4 = (f32[512]{0:T(512)S(1)}, f32[512]{0:T(512)}, u32[]{:S(2)}) copy-start(f32[512]{0:T(512)} %param.9) | copy-start | bytes 6148
  26.1 5.8 %collective-permute-start.1 = (f32[256,512]{1,0:T(8,128)S(1)}, f32[256,512]{1,0:T(8,128)S(1)}, u32[]{:S(2)}, u32[]{:S(2)}) collective-permute-start(f32[256,512]{1,0:T(8,128)S(1)} %bitcast.12), channel_id=1, source_target_pairs={{0,1},{1,0},{2,3},{3,2},{4,5},{5,4},{6,7},{7,6},{8,9},{9,8},{10,11... | collective-permute-start | bytes 1572872 | tf_op jit(solution)/shard_map/ppermute | solution.py:172
  28.4 3.8 %collective-permute-start.2 = (f32[256,512]{1,0:T(8,128)S(1)}, f32[256,512]{1,0:T(8,128)S(1)}, u32[]{:S(2)}, u32[]{:S(2)}) collective-permute-start(f32[256,512]{1,0:T(8,128)S(1)} %collective-permute-done.refs_1_), channel_id=1, source_target_pairs={{0,1},{1,0},{2,3},{3,2},{4,5},{5,4},{6,7},{7,6},{8,9},{9,8},{10,11... | collective-permute-start | bytes 1572872 | tf_op jit(solution)/shard_map/ppermute | solution.py:172
  30.5 0.8 %copy-start.1 = (f32[256,512]{1,0:T(8,128)}, f32[256,512]{1,0:T(8,128)S(1)}, u32[]{:S(2)}) copy-start(f32[256,512]{1,0:T(8,128)S(1)} %collective-permute-done.refs_1_) | copy-start | bytes 1572868
  31.9 0.7 %copy-start.5 = (s32[8]{0:T(128)S(1)}, s32[8]{0:T(128)}, u32[]{:S(2)}) copy-start(s32[8]{0:T(128)} %count_ref.1) | copy-start | bytes 100
  32.6 1.0 %copy-start.2 = (f32[256,512]{1,0:T(8,128)S(1)}, f32[256,512]{1,0:T(8,128)}, u32[]{:S(2)}) copy-start(f32[256,512]{1,0:T(8,128)} %copy-done.1) | copy-start | bytes 1572868

commit v5 on v4

--- a/solution.py
+++ b/solution.py
@@ -11,7 +11,6 @@
 GAMMA = 3
 CORES = 2
 SLABS = 2
-CHUNKS = 4
 RING = 8
 VMEM_BYTES = 48 * 1024 * 1024
 
@@ -23,33 +22,32 @@
 
 
 def regroup_kernel(place_order, cells_ref, out_ref, ready, sems):
-    pairs, all_lines, _ = cells_ref.shape
-    places, lines, _ = out_ref.shape
-    parts = lines // pairs
-    chunks = sems.shape[0]
-    places_each, lines_each = places // chunks, all_lines // chunks
+    pairs = cells_ref.shape[0]
+    rows, columns, lines, _ = ready.shape
+    parts = lines // pairs // SLABS
     copies = []
-    for chunk in range(chunks):
+    for row in range(rows):
         for pair in range(pairs):
-            line = (pair % CORES) * (lines // CORES) + (pair // CORES) * parts
-            for part in range(parts):
-                ready[chunk, :, line + part, :] = cells_ref[
-                    pair, pl.ds(chunk * lines_each + part, places_each, stride=parts), :
-                ]
-            for index in range(places_each):
-                place = place_order[chunk * places_each + index]
-                if place != chunk * places_each + index:
-                    ready[chunk, index, line : line + parts, :] = cells_ref[
-                        pair, place * parts : (place + 1) * parts, :
+            for side in range(SLABS):
+                line = ((pair % CORES * pairs + pair // CORES * CORES) // CORES * SLABS + side) * parts
+                first = (row * SLABS + side) * columns * parts
+                for part in range(parts):
+                    ready[row, :, line + part, :] = cells_ref[
+                        pair, pl.ds(first + part, columns, stride=parts), :
                     ]
+                for index in range(columns):
+                    place = place_order[row * columns + index]
+                    if place != row * columns + index:
+                        slab = (place // columns * SLABS + side) * columns + place % columns
+                        ready[row, index, line : line + parts, :] = cells_ref[
+                            pair, slab * parts : (slab + 1) * parts, :
+                        ]
         copies.append(
             pltpu.make_async_copy(
-                ready.at[chunk],
-                out_ref.at[pl.ds(chunk * places_each, places_each)],
-                sems.at[chunk],
+                ready.at[row], out_ref.at[pl.ds(row * columns, columns)], sems.at[row]
             )
         )
-        copies[chunk].start()
+        copies[row].start()
     for copy in copies:
         copy.wait()
 
@@ -59,21 +57,29 @@
     return high, (value - high.astype(jnp.float32)).astype(jnp.bfloat16)
 
 
-def weights_kernel(count_ref, pair_energy_ref, virt_energy_ref, *refs):
-    held_refs, (high_ref, low_ref, gap_ref) = refs[: CORES * SLABS], refs[CORES * SLABS :]
-    cells, virt = held_refs[0].shape
-    parts = cells // VMAX
-    cell = lax.broadcasted_iota(jnp.int32, (cells, virt), 0)
-    for turn, held_ref in enumerate(held_refs):
-        irrep = jnp.bitwise_xor(lax.axis_index("contract"), turn // SLABS)
-        slab = jnp.bitwise_xor(lax.axis_index("redist"), turn % SLABS)
-        row, col = slab * parts + cell // VMAX, cell % VMAX
+def put_weights(moves, count_ref, held_refs, high_ref, low_ref):
+    for (core_move, slab_move), held_ref in zip(moves, held_refs):
+        cells, virt = held_ref.shape
+        irrep = jnp.bitwise_xor(lax.axis_index("contract"), core_move)
+        slab = jnp.bitwise_xor(lax.axis_index("redist"), slab_move)
+        cell = lax.broadcasted_iota(jnp.int32, (cells, virt), 0)
+        row, col = slab * (cells // VMAX) + cell // VMAX, cell % VMAX
         live = (row < count_ref[irrep]) & (col < count_ref[jnp.bitwise_xor(irrep, GAMMA)])
         high, low = split_bf16(jnp.where(live, 0.5 * held_ref[...], 0.0))
-        place = pl.multiple_of((irrep % CORES * SLABS + slab % SLABS) * cells, cells)
+        block = irrep % CORES * SLABS + slab // RING % SLABS
+        place = pl.multiple_of(block * cells, cells)
         high_ref[pl.ds(place, cells), :] = high
         low_ref[pl.ds(place, cells), :] = low
+
+
+def weights_kernel(moves, count_ref, pair_energy_ref, virt_energy_ref, *refs):
+    held_refs, (high_ref, low_ref, gap_ref) = refs[: len(moves)], refs[len(moves) :]
+    put_weights(moves, count_ref, held_refs, high_ref, low_ref)
     gap_ref[...] = virt_energy_ref[...] - pair_energy_ref[0]
+
+
+def last_weights_kernel(move, count_ref, held_ref, _, __, high_ref, low_ref):
+    put_weights([move], count_ref, [held_ref], high_ref, low_ref)
 
 
 def ladder_kernel(chip_order, rows_ref, high_ref, low_ref, out_ref):
@@ -114,7 +120,7 @@
     out_ref[...] = (total[:blocks] + total[blocks:]) / gap_ref[...]
 
 
-def call(kernel, outs, in_memory, cost=None, out_memory=pltpu.VMEM, scratch=()):
+def call(kernel, outs, in_memory, cost=None, out_memory=pltpu.VMEM, scratch=(), aliases={}):
     single = not isinstance(outs, list)
     shapes = [jax.ShapeDtypeStruct(*out) for out in ([outs] if single else outs)]
     specs = [pl.BlockSpec(memory_space=out_memory) for _ in shapes]
@@ -125,6 +131,7 @@
         out_specs=specs[0] if single else specs,
         scratch_shapes=scratch,
         cost_estimate=cost,
+        input_output_aliases=aliases,
         compiler_params=pltpu.CompilerParams(vmem_limit_bytes=VMEM_BYTES),
     )
 
@@ -140,11 +147,12 @@
     f32, bf16 = jnp.float32, jnp.bfloat16
 
     def device(place, side, chip, core):
-        slab = place * SLABS + (side ^ (place // 2 % 2))
+        row, column = divmod(place, RING)
+        slab = (row * SLABS + (side ^ ((row + 1) // 2 % 2))) * RING + column
         return slab * owners + chip * CORES + core
 
-    columns = RING // SLABS
-    place_order = first_swapped(places, places // 2 + columns // 2)
+    rows = places // RING
+    place_order = first_swapped(places, rows // 2 * RING + RING // 2)
     chip_order = first_swapped(chips, chips // 2)
     same_chip = [
         [device(place, side, chip, core) for place in place_order for core in range(CORES)]
@@ -167,13 +175,14 @@
             tiled=True,
         )
 
-    def swap(block, axis):
+    def swap(block, axis, move):
         count = lax.axis_size(axis)
-        return lax.ppermute(block, axis, [(index, index ^ 1) for index in range(count)])
+        return lax.ppermute(block, axis, [(index, index ^ move) for index in range(count)])
 
     own = integrals.reshape(cells, virt)
-    held = [own, swap(own, "redist")]
-    held = held + [swap(block, "contract") for block in held]
+    held = {(0, 0): own, (0, RING): swap(own, "redist", RING)}
+    held |= {(1, move): swap(block, "contract", 1) for (_, move), block in held.items()}
+    last_move, last_block = held.popitem()
 
     all_lines = cells_all // VMAX
     lines = pairs * all_lines // places
@@ -183,21 +192,32 @@
         [vmem],
         out_memory=pltpu.HBM,
         scratch=[
-            pltpu.VMEM((CHUNKS, places // CHUNKS, lines, VMAX), f32),
-            pltpu.SemaphoreType.DMA((CHUNKS,)),
+            pltpu.VMEM((rows, RING, lines, VMAX), f32),
+            pltpu.SemaphoreType.DMA((rows,)),
         ],
     )(amplitudes.reshape(pairs, all_lines, VMAX))
     arrived = exchange(grouped.reshape(places * CORES, lines // CORES, VMAX), same_chip)
 
     depth = CORES * SLABS * cells
+    weights = ((depth, virt), bf16)
+
+    def cost(blocks_made):
+        amount = blocks_made * cells * virt
+        return pl.CostEstimate(flops=10 * amount, bytes_accessed=8 * amount, transcendentals=0)
+
     high, low, gap = call(
-        weights_kernel,
-        [((depth, virt), bf16), ((depth, virt), bf16), ((blocks, VMAX), f32)],
+        functools.partial(weights_kernel, list(held)),
+        [weights, weights, ((blocks, VMAX), f32)],
         [smem, smem, vmem] + [vmem] * len(held),
-        cost=pl.CostEstimate(
-            flops=10 * depth * virt, bytes_accessed=8 * depth * virt, transcendentals=0
-        ),
-    )(irrep_count, pair_energy, virt_energy.reshape(blocks, VMAX), *held)
+        cost=cost(len(held)),
+    )(irrep_count, pair_energy, virt_energy.reshape(blocks, VMAX), *held.values())
+    high, low = call(
+        functools.partial(last_weights_kernel, last_move),
+        [weights, weights],
+        [smem, vmem, vmem, vmem],
+        cost=cost(1),
+        aliases={2: 0, 3: 1},
+    )(irrep_count, last_block, high, low)
 
     partial = call(
         functools.partial(ladder_kernel, chip_order),

time: 62 us -> 61.2 us (0.987)
  local copies, waits for them, and re-layouts: 3.22 us -> 1.68 us
  starting transfers between devices: 28.4 us -> 27.1 us
  Pallas kernels: 3.69 us -> 4.72 us
  waiting for transfers between devices: 4.21 us -> 4.87 us
    all_to_all x1, starting transfers between devices: 20 us -> 17.9 us  [exchange(): lax.all_to_all(blocks_out, ('redist', 'contract'), split_axis=0, concat_a...]
    unnamed x12 -> x8, local copies, waits for them, and re-layouts: 3.22 us -> 1.68 us
    pallas_call x1 -> x2, Pallas kernels: 1.14 us -> 2.16 us  [the longest x1 1.49 us: body(): call(functools.partial(weights_kernel, list(held)), [weights, weights, ((...]
    all_to_all x1, waiting for transfers between devices: 3.92 us -> 4.86 us  [exchange(): lax.all_to_all(blocks_out, ('redist', 'contract'), split_axis=0, concat_a...]
    ppermute x3, starting transfers between devices: 8.35 us -> 9.15 us  [swap(): lax.ppermute(block, axis, [(index, index ^ move) for index in range(count)])]
  transfers between devices with their start and end apart: 4 -> 4, of which waited for: 2 -> 1; matrix products, arithmetic and copies ran while one was open for 0% -> 0% of each run, Pallas kernels for 3% -> 5%
where the time goes in v5:
time: 61.2 us; the launch traced here: 60.5 us
  starting transfers between devices  27.1 us (44%)
  blocking collectives  21.4 us (35%)
  waiting for transfers between devices  4.87 us (8%)
  Pallas kernels  4.72 us (8%)
  local copies, waits for them, and re-layouts  1.68 us (3%)
  between operations  0.78 us (1%)
    all_to_all x1, blocking collectives, exchange(): lax.all_to_all(blocks_out, ('redist', 'contract'), split_axis=0, concat_a...  21.4 us
    all_to_all x1, starting transfers between devices, exchange(): lax.all_to_all(blocks_out, ('redist', 'contract'), split_axis=0, concat_a...  17.9 us
    ppermute x3, starting transfers between devices, swap(): lax.ppermute(block, axis, [(index, index ^ move) for index in range(count)])  9.15 us
    all_to_all x1, waiting for transfers between devices, exchange(): lax.all_to_all(blocks_out, ('redist', 'contract'), split_axis=0, concat_a...  4.86 us
    unnamed x8, local copies, waits for them, and re-layouts  1.68 us
    pallas_call x1, Pallas kernels, body(): call(functools.partial(weights_kernel, list(held)), [weights, weights, ((...  1.49 us
  transfers between devices with their start and end apart: 4, of which 1 were waited for; matrix products, arithmetic and copies ran while one was open for 0% of the time, Pallas kernels for 5%

profile of v5, /device:TPU:1, one launch (start us, length us, event | category | flops | bytes accessed | tf_op | source)
XLA Modules:
  0.0 60.5 jit_solution(612618470717602299)
XLA Ops:
  0.0 4.8 %collective-permute-start = (f32[256,512]{1,0:T(8,128)}, f32[256,512]{1,0:T(8,128)}, u32[]{:S(2)}, u32[]{:S(2)}) collective-permute-start(f32[256,512]{1,0:T(8,128)} %bitcast.12), channel_id=1, source_target_pairs={{0,64},{8,72},{16,80},{24,88},{32,96},{40,104},{48,112},{56,120},{... | collective-permute-start | bytes 1572872 | tf_op jit(solution)/shard_map/ppermute | solution.py:180
  4.8 0.0 copy-start
  4.8 1.0 %copy-done = f32[8,1,16384]{2,1,0:T(1,128)S(1)} copy-done((f32[8,1,16384]{2,1,0:T(1,128)S(1)}, f32[8,1,16384]{2,1,0:T(1,128)}, u32[]{:S(2)}) %copy-start) | copy-done | bytes 524312
  5.9 1.0 %shard_map.55 = f32[32,32,128]{2,1,0:T(8,128)} custom-call(f32[8,128,128]{2,1,0:T(8,128)S(1)} %bitcast.11), custom_call_target="tpu_custom_call" | custom-call | tf_op jit(solution)/shard_map/pallas_call | solution.py:189
  6.9 0.0 copy-start.1
  6.9 17.9 %all-to-all-start = ((f32[64,16,128]{2,1,0:T(8,128)}), f32[64,16,128]{2,1,0:T(8,128)S(1)}, u32[]{:S(2)}, u32[]{:S(2)}) async-start(f32[64,16,128]{2,1,0:T(8,128)} %bitcast.1), calls=%async_computation | async-start | bytes 1048576 | tf_op jit(solution)/shard_map/all_to_all | solution.py:169
  24.8 0.0 copy-done.1
  24.8 0.0 copy-start.2
  24.8 2.3 %collective-permute-start.2 = (f32[256,512]{1,0:T(8,128)S(1)}, f32[256,512]{1,0:T(8,128)S(1)}, u32[]{:S(2)}, u32[]{:S(2)}) collective-permute-start(f32[256,512]{1,0:T(8,128)S(1)} %bitcast.13), channel_id=1, source_target_pairs={{0,1},{1,0},{2,3},{3,2},{4,5},{5,4},{6,7},{7,6},{8,9},{9,8},{10,11... | collective-permute-start | bytes 1572872 | tf_op jit(solution)/shard_map/ppermute | solution.py:180
  27.1 0.0 collective-permute-done.refs_1_
  27.1 2.1 %collective-permute-start.1 = (f32[256,512]{1,0:T(8,128)}, f32[256,512]{1,0:T(8,128)S(1)}, u32[]{:S(2)}, u32[]{:S(2)}) collective-permute-start(f32[256,512]{1,0:T(8,128)} %collective-permute-done.refs_1_), channel_id=1, source_target_pairs={{0,1},{1,0},{2,3},{3,2},{4,5},{5,4},{6,7},{7,6},{8,9},{9,8},{10,11... | collective-permute-start | bytes 1572872 | tf_op jit(solution)/shard_map/ppermute | solution.py:180
  29.8 0.0 copy-start.3
  29.9 0.0 collective-permute-done.2.refs_2_
  29.9 0.0 copy-done.2
  29.9 0.6 %copy-done.3 = s32[8]{0:T(128)S(1)} copy-done((s32[8]{0:T(128)S(1)}, s32[8]{0:T(128)}, u32[]{:S(2)}) %copy-start.3) | copy-done | bytes 56
  30.5 1.5 %shard_map.56 = (bf16[1024,512]{1,0:T(8,128)(2,1)S(1)}, bf16[1024,512]{1,0:T(8,128)(2,1)S(1)}, f32[4,128]{1,0:T(4,128)S(1)}) custom-call(s32[8]{0:T(128)S(1)} %copy-done.3, f32[1]{0:T(128)S(6)} %copy.10.pair_energy_ref, f32[4,128]{1,0:T(4,128)S(1)} %bitcast.15, f32[256,512]{1,0:T(8,128)S(1)} %bitcast.14, f32[256,512]{1,0:T(8,128)} %collective-permute-done.refs_1_, ...), custom_call_target="tpu_custom_call" | custom-call | flops 3932160 | bytes 3145728 | tf_op jit(solution)/shard_map/pallas_call | solution.py:208
  32.0 0.0 collective-permute-done.1.held_ref
  32.0 0.7 %shard_map.57 = (bf16[1024,512]{1,0:T(8,128)(2,1)S(1)}, bf16[1024,512]{1,0:T(8,128)(2,1)S(1)}) custom-call(s32[8]{0:T(128)S(1)} %copy-done.3, f32[256,512]{1,0:T(8,128)S(1)} %collective-permute-done.1.held_ref, bf16[1024,512]{1,0:T(8,128)(2,1)S(1)} %get-tuple-element.10._, ...), custom_call_target="tpu_custom_call", output_to_operand_aliasing={{0}: (2, {}), {1}: (3, {})} | custom-call | flops 1310720 | bytes 1048576 | tf_op jit(solution)/shard_map/pallas_call | solution.py:214
  32.7 4.9 %all-to-all-done = f32[64,16,128]{2,1,0:T(8,128)S(1)} async-done(((f32[64,16,128]{2,1,0:T(8,128)}), f32[64,16,128]{2,1,0:T(8,128)S(1)}, u32[]{:S(2)}, u32[]{:S(2)}) %all-to-all-start) | async-done | bytes 524320 | tf_op jit(solution)/shard_map/all_to_all | solution.py:169
  37.5 0.9 %shard_map.58 = f32[32,16,128]{2,1,0:T(8,128)S(1)} custom-call(f32[32,32,128]{2,1,0:T(8,128)S(1)} %bitcast.8, bf16[1024,512]{1,0:T(8,128)(2,1)S(1)} %get-tuple-element.12.high_ref, bf16[1024,512]{1,0:T(8,128)(2,1)S(1)} %get-tuple-element.13.low_ref), custom_call_target="tpu_custom_call" | custom-call | tf_op jit(solution)/shard_map/pallas_call | solution.py:222
  38.5 21.4 %all_to_all.10 = f32[128,4,128]{2,1,0:T(4,128)S(1)} all-to-all(f32[128,4,128]{2,1,0:T(4,128)S(1)} %bitcast.10), channel_id=1, replica_groups={{356,354,352,358,12,10,8,14,20,18,16,22,28,26,24,30,36,34,32,38,44,42,4..., dimensions={0} | all-to-all | bytes 524288 | tf_op jit(solution)/shard_map/all_to_all | solution.py:169
  59.9 0.6 %shard_map.59 = f32[4,128]{1,0:T(4,128)} custom-call(f32[512,128]{1,0:T(8,128)S(1)} %bitcast.9, f32[4,128]{1,0:T(4,128)S(1)} %get-tuple-element.14.gap_ref), custom_call_target="tpu_custom_call" | custom-call | tf_op jit(solution)/shard_map/pallas_call | solution.py:228
Async XLA Ops:
  0.0 27.1 %collective-permute-start = (f32[256,512]{1,0:T(8,128)}, f32[256,512]{1,0:T(8,128)}, u32[]{:S(2)}, u32[]{:S(2)}) collective-permute-start(f32[256,512]{1,0:T(8,128)} %bitcast.12), channel_id=1, source_target_pairs={{0,64},{8,72},{16,80},{24,88},{32,96},{40,104},{48,112},{56,120},{... | collective-permute-start | bytes 1572872 | tf_op jit(solution)/shard_map/ppermute | solution.py:180
  4.8 1.0 %copy-start = (f32[8,1,16384]{2,1,0:T(1,128)S(1)}, f32[8,1,16384]{2,1,0:T(1,128)}, u32[]{:S(2)}) copy-start(f32[8,1,16384]{2,1,0:T(1,128)} %param.5) | copy-start | bytes 1572868
  6.9 17.9 %copy-start.1 = (f32[1,256,512]{2,1,0:T(8,128)S(1)}, f32[1,256,512]{2,1,0:T(8,128)}, u32[]{:S(2)}) copy-start(f32[1,256,512]{2,1,0:T(8,128)} %param.6) | copy-start | bytes 1572868
  6.9 30.7 %all-to-all-start = ((f32[64,16,128]{2,1,0:T(8,128)}), f32[64,16,128]{2,1,0:T(8,128)S(1)}, u32[]{:S(2)}, u32[]{:S(2)}) async-start(f32[64,16,128]{2,1,0:T(8,128)} %bitcast.1), calls=%async_computation | async-start | bytes 1048576 | tf_op jit(solution)/shard_map/all_to_all | solution.py:169
  24.8 5.0 %copy-start.2 = (f32[512]{0:T(512)S(1)}, f32[512]{0:T(512)}, u32[]{:S(2)}) copy-start(f32[512]{0:T(512)} %param.9) | copy-start | bytes 6148
  24.8 5.0 %collective-permute-start.2 = (f32[256,512]{1,0:T(8,128)S(1)}, f32[256,512]{1,0:T(8,128)S(1)}, u32[]{:S(2)}, u32[]{:S(2)}) collective-permute-start(f32[256,512]{1,0:T(8,128)S(1)} %bitcast.13), channel_id=1, source_target_pairs={{0,1},{1,0},{2,3},{3,2},{4,5},{5,4},{6,7},{7,6},{8,9},{9,8},{10,11... | collective-permute-start | bytes 1572872 | tf_op jit(solution)/shard_map/ppermute | solution.py:180
  27.1 4.9 %collective-permute-start.1 = (f32[256,512]{1,0:T(8,128)}, f32[256,512]{1,0:T(8,128)S(1)}, u32[]{:S(2)}, u32[]{:S(2)}) collective-permute-start(f32[256,512]{1,0:T(8,128)} %collective-permute-done.refs_1_), channel_id=1, source_target_pairs={{0,1},{1,0},{2,3},{3,2},{4,5},{5,4},{6,7},{7,6},{8,9},{9,8},{10,11... | collective-permute-start | bytes 1572872 | tf_op jit(solution)/shard_map/ppermute | solution.py:180
  29.8 0.7 %copy-start.3 = (s32[8]{0:T(128)S(1)}, s32[8]{0:T(128)}, u32[]{:S(2)}) copy-start(s32[8]{0:T(128)} %count_ref.3) | copy-start | bytes 100

commit v6 on v5

--- a/solution.py
+++ b/solution.py
@@ -58,7 +58,7 @@
 
 
 def put_weights(moves, count_ref, held_refs, high_ref, low_ref):
-    for (core_move, slab_move), held_ref in zip(moves, held_refs):
+    for index, ((core_move, slab_move), held_ref) in enumerate(zip(moves, held_refs)):
         cells, virt = held_ref.shape
         irrep = jnp.bitwise_xor(lax.axis_index("contract"), core_move)
         slab = jnp.bitwise_xor(lax.axis_index("redist"), slab_move)
@@ -66,10 +66,8 @@
         row, col = slab * (cells // VMAX) + cell // VMAX, cell % VMAX
         live = (row < count_ref[irrep]) & (col < count_ref[jnp.bitwise_xor(irrep, GAMMA)])
         high, low = split_bf16(jnp.where(live, 0.5 * held_ref[...], 0.0))
-        block = irrep % CORES * SLABS + slab // RING % SLABS
-        place = pl.multiple_of(block * cells, cells)
-        high_ref[pl.ds(place, cells), :] = high
-        low_ref[pl.ds(place, cells), :] = low
+        high_ref[index * cells : (index + 1) * cells, :] = high
+        low_ref[index * cells : (index + 1) * cells, :] = low
 
 
 def weights_kernel(moves, count_ref, pair_energy_ref, virt_energy_ref, *refs):
@@ -78,35 +76,54 @@
     gap_ref[...] = virt_energy_ref[...] - pair_energy_ref[0]
 
 
-def last_weights_kernel(move, count_ref, held_ref, _, __, high_ref, low_ref):
+def last_weights_kernel(move, count_ref, held_ref, high_ref, low_ref):
     put_weights([move], count_ref, [held_ref], high_ref, low_ref)
 
 
-def ladder_kernel(chip_order, rows_ref, high_ref, low_ref, out_ref):
+def ladder_kernel(chip_order, moves, rows_ref, high_ref, low_ref, last_high_ref, last_low_ref, out_ref):
     places, lines, _ = rows_ref.shape
-    depth, virt = high_ref.shape
+    virt = high_ref.shape[1]
     blocks = virt // VMAX
     turns = out_ref.shape[1] // blocks
-    parts = depth // VMAX // CORES
-    rows = jnp.concatenate(
-        [
-            jnp.concatenate(
-                [
-                    rows_ref[:, (source * turns + turn) * parts + part, :]
-                    for source in range(CORES)
-                    for part in range(parts)
-                ],
-                axis=1,
-            )
-            for turn in range(turns)
-        ],
-        axis=0,
-    )
-    rows_high, rows_low = split_bf16(rows)
-    high, low = high_ref[...], low_ref[...]
-    total = jnp.dot(rows_high, low, preferred_element_type=jnp.float32)
-    total = total + jnp.dot(rows_low, high, preferred_element_type=jnp.float32)
-    total = total + jnp.dot(rows_high, high, preferred_element_type=jnp.float32)
+    parts = last_high_ref.shape[0] // VMAX
+    core = lax.axis_index("contract") % CORES
+    side = lax.axis_index("redist") // RING % SLABS
+
+    def arrived(source, slab_side):
+        return jnp.concatenate(
+            [
+                jnp.concatenate(
+                    [
+                        rows_ref[:, ((source * turns + turn) * SLABS + slab_side) * parts + part, :]
+                        for part in range(parts)
+                    ],
+                    axis=1,
+                )
+                for turn in range(turns)
+            ],
+            axis=0,
+        )
+
+    by_source = [[arrived(source, slab_side) for slab_side in range(SLABS)] for source in range(CORES)]
+    by_core = [
+        [jnp.where(core == 0, by_source[turn][place], by_source[1 - turn][place]) for place in range(SLABS)]
+        for turn in range(CORES)
+    ]
+    by_move = {
+        (turn, place * RING): jnp.where(side == 0, by_core[turn][place], by_core[turn][1 - place])
+        for turn in range(CORES)
+        for place in range(SLABS)
+    }
+    pieces = [by_move[move] for move in moves]
+    total = jnp.zeros((turns * places, virt), jnp.float32)
+    for rows, high, low in (
+        (pieces[-1], last_high_ref[...], last_low_ref[...]),
+        (jnp.concatenate(pieces[:-1], axis=1), high_ref[...], low_ref[...]),
+    ):
+        rows_high, rows_low = split_bf16(rows)
+        total = total + jnp.dot(rows_high, low, preferred_element_type=jnp.float32)
+        total = total + jnp.dot(rows_low, high, preferred_element_type=jnp.float32)
+        total = total + jnp.dot(rows_high, high, preferred_element_type=jnp.float32)
     for index, turn in enumerate(chip_order):
         for block in range(blocks):
             out_ref[:, index * blocks + block, :] = total[
@@ -120,7 +137,7 @@
     out_ref[...] = (total[:blocks] + total[blocks:]) / gap_ref[...]
 
 
-def call(kernel, outs, in_memory, cost=None, out_memory=pltpu.VMEM, scratch=(), aliases={}):
+def call(kernel, outs, in_memory, cost=None, out_memory=pltpu.VMEM, scratch=()):
     single = not isinstance(outs, list)
     shapes = [jax.ShapeDtypeStruct(*out) for out in ([outs] if single else outs)]
     specs = [pl.BlockSpec(memory_space=out_memory) for _ in shapes]
@@ -131,7 +148,6 @@
         out_specs=specs[0] if single else specs,
         scratch_shapes=scratch,
         cost_estimate=cost,
-        input_output_aliases=aliases,
         compiler_params=pltpu.CompilerParams(vmem_limit_bytes=VMEM_BYTES),
     )
 
@@ -198,32 +214,30 @@
     )(amplitudes.reshape(pairs, all_lines, VMAX))
     arrived = exchange(grouped.reshape(places * CORES, lines // CORES, VMAX), same_chip)
 
-    depth = CORES * SLABS * cells
-    weights = ((depth, virt), bf16)
-
-    def cost(blocks_made):
+    def weights(blocks_made):
         amount = blocks_made * cells * virt
-        return pl.CostEstimate(flops=10 * amount, bytes_accessed=8 * amount, transcendentals=0)
-
+        return (
+            [((blocks_made * cells, virt), bf16)] * 2,
+            pl.CostEstimate(flops=10 * amount, bytes_accessed=8 * amount, transcendentals=0),
+        )
+
+    outs, cost = weights(len(held))
     high, low, gap = call(
         functools.partial(weights_kernel, list(held)),
-        [weights, weights, ((blocks, VMAX), f32)],
+        [*outs, ((blocks, VMAX), f32)],
         [smem, smem, vmem] + [vmem] * len(held),
-        cost=cost(len(held)),
+        cost=cost,
     )(irrep_count, pair_energy, virt_energy.reshape(blocks, VMAX), *held.values())
-    high, low = call(
-        functools.partial(last_weights_kernel, last_move),
-        [weights, weights],
-        [smem, vmem, vmem, vmem],
-        cost=cost(1),
-        aliases={2: 0, 3: 1},
-    )(irrep_count, last_block, high, low)
+    outs, cost = weights(1)
+    last_high, last_low = call(
+        functools.partial(last_weights_kernel, last_move), outs, [smem, vmem], cost=cost
+    )(irrep_count, last_block)
 
     partial = call(
-        functools.partial(ladder_kernel, chip_order),
+        functools.partial(ladder_kernel, chip_order, [*held, last_move]),
         ((places, chips * blocks, VMAX), f32),
-        [vmem] * 3,
-    )(arrived.reshape(places, lines, VMAX), high, low)
+        [vmem] * 5,
+    )(arrived.reshape(places, lines, VMAX), high, low, last_high, last_low)
     partial = exchange(partial.reshape(places * chips, blocks, VMAX), same_core)
     delta = call(finish_kernel, ((blocks, VMAX), f32), [vmem] * 2)(
         partial.reshape(-1, VMAX), gap

time: 61.2 us -> 61.2 us (level)
  transfers between devices with their start and end apart: 4 -> 4, of which waited for: 1 -> 1; matrix products, arithmetic and copies ran while one was open for 0% -> 0% of each run, Pallas kernels for 5% -> 4%
where the time goes in v6:
time: 61.2 us; the launch traced here: 60.6 us
  starting transfers between devices  27.1 us (44%)
  blocking collectives  21.4 us (35%)
  waiting for transfers between devices  5.44 us (9%)
  Pallas kernels  4.21 us (7%)
  local copies, waits for them, and re-layouts  1.68 us (3%)
  between operations  0.78 us (1%)
    all_to_all x1, blocking collectives, exchange(): lax.all_to_all(blocks_out, ('redist', 'contract'), split_axis=0, concat_a...  21.4 us
    all_to_all x1, starting transfers between devices, exchange(): lax.all_to_all(blocks_out, ('redist', 'contract'), split_axis=0, concat_a...  17.9 us
    ppermute x3, starting transfers between devices, swap(): lax.ppermute(block, axis, [(index, index ^ move) for index in range(count)])  9.15 us
    all_to_all x1, waiting for transfers between devices, exchange(): lax.all_to_all(blocks_out, ('redist', 'contract'), split_axis=0, concat_a...  5.43 us
    unnamed x8, local copies, waits for them, and re-layouts  1.68 us
  transfers between devices with their start and end apart: 4, of which 1 were waited for; matrix products, arithmetic and copies ran while one was open for 0% of the time, Pallas kernels for 4%

profile of v6, /device:TPU:1, one launch (start us, length us, event | category | flops | bytes accessed | tf_op | source)
XLA Modules:
  0.0 60.6 jit_solution(4923420567741493117)
XLA Ops:
  0.0 4.8 %collective-permute-start = (f32[256,512]{1,0:T(8,128)}, f32[256,512]{1,0:T(8,128)S(1)}, u32[]{:S(2)}, u32[]{:S(2)}) collective-permute-start(f32[256,512]{1,0:T(8,128)} %bitcast.12), channel_id=1, source_target_pairs={{0,64},{8,72},{16,80},{24,88},{32,96},{40,104},{48,112},{56,120},{... | collective-permute-start | bytes 1572872 | tf_op jit(solution)/shard_map/ppermute | solution.py:196
  4.8 0.0 copy-start
  4.8 1.0 %copy-done = f32[8,1,16384]{2,1,0:T(1,128)S(1)} copy-done((f32[8,1,16384]{2,1,0:T(1,128)S(1)}, f32[8,1,16384]{2,1,0:T(1,128)}, u32[]{:S(2)}) %copy-start) | copy-done | bytes 524312
  5.9 1.0 %shard_map.55 = f32[32,32,128]{2,1,0:T(8,128)} custom-call(f32[8,128,128]{2,1,0:T(8,128)S(1)} %bitcast.11), custom_call_target="tpu_custom_call" | custom-call | tf_op jit(solution)/shard_map/pallas_call | solution.py:205
  6.9 0.0 copy-start.1
  6.9 17.9 %all-to-all-start = ((f32[64,16,128]{2,1,0:T(8,128)}), f32[64,16,128]{2,1,0:T(8,128)S(1)}, u32[]{:S(2)}, u32[]{:S(2)}) async-start(f32[64,16,128]{2,1,0:T(8,128)} %bitcast.1), calls=%async_computation | async-start | bytes 1048576 | tf_op jit(solution)/shard_map/all_to_all | solution.py:185
  24.8 0.0 copy-done.1
  24.8 0.0 copy-start.2
  24.8 2.3 %collective-permute-start.1 = (f32[256,512]{1,0:T(8,128)S(1)}, f32[256,512]{1,0:T(8,128)S(1)}, u32[]{:S(2)}, u32[]{:S(2)}) collective-permute-start(f32[256,512]{1,0:T(8,128)S(1)} %bitcast.13), channel_id=1, source_target_pairs={{0,1},{1,0},{2,3},{3,2},{4,5},{5,4},{6,7},{7,6},{8,9},{9,8},{10,11... | collective-permute-start | bytes 1572872 | tf_op jit(solution)/shard_map/ppermute | solution.py:196
  27.1 0.0 collective-permute-done.refs_1_
  27.1 2.1 %collective-permute-start.2 = (f32[256,512]{1,0:T(8,128)S(1)}, f32[256,512]{1,0:T(8,128)S(1)}, u32[]{:S(2)}, u32[]{:S(2)}) collective-permute-start(f32[256,512]{1,0:T(8,128)S(1)} %collective-permute-done.refs_1_), channel_id=1, source_target_pairs={{0,1},{1,0},{2,3},{3,2},{4,5},{5,4},{6,7},{7,6},{8,9},{9,8},{10,11... | collective-permute-start | bytes 1572872 | tf_op jit(solution)/shard_map/ppermute | solution.py:196
  29.8 0.0 copy-start.3
  29.9 0.0 collective-permute-done.1.refs_2_
  29.9 0.0 copy-done.2
  29.9 0.6 %copy-done.3 = s32[8]{0:T(128)S(1)} copy-done((s32[8]{0:T(128)S(1)}, s32[8]{0:T(128)}, u32[]{:S(2)}) %copy-start.3) | copy-done | bytes 56
  30.5 0.9 %shard_map.56 = (bf16[768,512]{1,0:T(8,128)(2,1)S(1)}, bf16[768,512]{1,0:T(8,128)(2,1)S(1)}, f32[4,128]{1,0:T(4,128)S(1)}) custom-call(s32[8]{0:T(128)S(1)} %copy-done.3, f32[1]{0:T(128)S(6)} %copy.6.pair_energy_ref, f32[4,128]{1,0:T(4,128)S(1)} %bitcast.15, f32[256,512]{1,0:T(8,128)S(1)} %bitcast.14, f32[256,512]{1,0:T(8,128)S(1)} %collective-permute-done.refs_1_, ...), custom_call_target="tpu_custom_call" | custom-call | flops 3932160 | bytes 3145728 | tf_op jit(solution)/shard_map/pallas_call | solution.py:225
  31.4 0.0 collective-permute-done.2.held_ref
  31.4 0.7 %shard_map.57 = (bf16[256,512]{1,0:T(8,128)(2,1)S(1)}, bf16[256,512]{1,0:T(8,128)(2,1)S(1)}) custom-call(s32[8]{0:T(128)S(1)} %copy-done.3, f32[256,512]{1,0:T(8,128)S(1)} %collective-permute-done.2.held_ref), custom_call_target="tpu_custom_call" | custom-call | flops 1310720 | bytes 1048576 | tf_op jit(solution)/shard_map/pallas_call | solution.py:232
  32.1 5.4 %all-to-all-done = f32[64,16,128]{2,1,0:T(8,128)S(1)} async-done(((f32[64,16,128]{2,1,0:T(8,128)}), f32[64,16,128]{2,1,0:T(8,128)S(1)}, u32[]{:S(2)}, u32[]{:S(2)}) %all-to-all-start) | async-done | bytes 524320 | tf_op jit(solution)/shard_map/all_to_all | solution.py:185
  37.5 1.0 %shard_map.58 = f32[32,16,128]{2,1,0:T(8,128)S(1)} custom-call(f32[32,32,128]{2,1,0:T(8,128)S(1)} %bitcast.8, bf16[768,512]{1,0:T(8,128)(2,1)S(1)} %get-tuple-element.10.high_ref, bf16[768,512]{1,0:T(8,128)(2,1)S(1)} %get-tuple-element.11.low_ref, bf16[256,512]{1,0:T(8,128)(2,1)S(1)} %get-tuple-element.12.last_high_ref, ...), custom_call_target="tpu_custom_call" | custom-call | tf_op jit(solution)/shard_map/pallas_call | solution.py:236
  38.5 21.4 %all_to_all.10 = f32[128,4,128]{2,1,0:T(4,128)S(1)} all-to-all(f32[128,4,128]{2,1,0:T(4,128)S(1)} %bitcast.10), channel_id=1, replica_groups={{356,354,352,358,12,10,8,14,20,18,16,22,28,26,24,30,36,34,32,38,44,42,4..., dimensions={0} | all-to-all | bytes 524288 | tf_op jit(solution)/shard_map/all_to_all | solution.py:185
  59.9 0.6 %shard_map.59 = f32[4,128]{1,0:T(4,128)} custom-call(f32[512,128]{1,0:T(8,128)S(1)} %bitcast.9, f32[4,128]{1,0:T(4,128)S(1)} %get-tuple-element.14.gap_ref), custom_call_target="tpu_custom_call" | custom-call | tf_op jit(solution)/shard_map/pallas_call | solution.py:242
Async XLA Ops:
  0.0 27.1 %collective-permute-start = (f32[256,512]{1,0:T(8,128)}, f32[256,512]{1,0:T(8,128)S(1)}, u32[]{:S(2)}, u32[]{:S(2)}) collective-permute-start(f32[256,512]{1,0:T(8,128)} %bitcast.12), channel_id=1, source_target_pairs={{0,64},{8,72},{16,80},{24,88},{32,96},{40,104},{48,112},{56,120},{... | collective-permute-start | bytes 1572872 | tf_op jit(solution)/shard_map/ppermute | solution.py:196
  4.8 1.0 %copy-start = (f32[8,1,16384]{2,1,0:T(1,128)S(1)}, f32[8,1,16384]{2,1,0:T(1,128)}, u32[]{:S(2)}) copy-start(f32[8,1,16384]{2,1,0:T(1,128)} %param.5) | copy-start | bytes 1572868
  6.9 17.9 %copy-start.1 = (f32[1,256,512]{2,1,0:T(8,128)S(1)}, f32[1,256,512]{2,1,0:T(8,128)}, u32[]{:S(2)}) copy-start(f32[1,256,512]{2,1,0:T(8,128)} %param.6) | copy-start | bytes 1572868
  6.9 30.7 %all-to-all-start = ((f32[64,16,128]{2,1,0:T(8,128)}), f32[64,16,128]{2,1,0:T(8,128)S(1)}, u32[]{:S(2)}, u32[]{:S(2)}) async-start(f32[64,16,128]{2,1,0:T(8,128)} %bitcast.1), calls=%async_computation | async-start | bytes 1048576 | tf_op jit(solution)/shard_map/all_to_all | solution.py:185
  24.8 5.0 %copy-start.2 = (f32[512]{0:T(512)S(1)}, f32[512]{0:T(512)}, u32[]{:S(2)}) copy-start(f32[512]{0:T(512)} %param.9) | copy-start | bytes 6148
  24.8 5.0 %collective-permute-start.1 = (f32[256,512]{1,0:T(8,128)S(1)}, f32[256,512]{1,0:T(8,128)S(1)}, u32[]{:S(2)}, u32[]{:S(2)}) collective-permute-start(f32[256,512]{1,0:T(8,128)S(1)} %bitcast.13), channel_id=1, source_target_pairs={{0,1},{1,0},{2,3},{3,2},{4,5},{5,4},{6,7},{7,6},{8,9},{9,8},{10,11... | collective-permute-start | bytes 1572872 | tf_op jit(solution)/shard_map/ppermute | solution.py:196
  27.1 4.3 %collective-permute-start.2 = (f32[256,512]{1,0:T(8,128)S(1)}, f32[256,512]{1,0:T(8,128)S(1)}, u32[]{:S(2)}, u32[]{:S(2)}) collective-permute-start(f32[256,512]{1,0:T(8,128)S(1)} %collective-permute-done.refs_1_), channel_id=1, source_target_pairs={{0,1},{1,0},{2,3},{3,2},{4,5},{5,4},{6,7},{7,6},{8,9},{9,8},{10,11... | collective-permute-start | bytes 1572872 | tf_op jit(solution)/shard_map/ppermute | solution.py:196
  29.8 0.7 %copy-start.3 = (s32[8]{0:T(128)S(1)}, s32[8]{0:T(128)}, u32[]{:S(2)}) copy-start(s32[8]{0:T(128)} %count_ref.3) | copy-start | bytes 100

commit v7 on v6

--- a/solution.py
+++ b/solution.py
@@ -13,6 +13,7 @@
 SLABS = 2
 RING = 8
 VMEM_BYTES = 48 * 1024 * 1024
+ALL_VMEM_BYTES = 63000000
 
 
 def first_swapped(count, first):
@@ -21,33 +22,48 @@
     return order
 
 
-def regroup_kernel(place_order, cells_ref, out_ref, ready, sems):
+def regroup_kernel(place_order, cells_ref, out_ref, held, ready, in_sems, out_sems):
     pairs = cells_ref.shape[0]
     rows, columns, lines, _ = ready.shape
     parts = lines // pairs // SLABS
-    copies = []
-    for row in range(rows):
+    row_lines = SLABS * columns * parts
+    arrivals = [
+        pltpu.make_async_copy(
+            cells_ref.at[:, pl.ds(row * row_lines, row_lines), :], held.at[row], in_sems.at[row]
+        )
+        for row in range(rows)
+    ]
+    swapped = [row for row in range(rows) if place_order[row * columns] != row * columns]
+    swapped += [place_order[row * columns] // columns for row in swapped]
+    turns = sorted(range(rows), key=lambda row: row in swapped)
+    for row in turns:
+        arrivals[row].start()
+    copies, waited = [], set()
+    for row in turns:
+        for needed in swapped if row in swapped else [row]:
+            if needed not in waited:
+                arrivals[needed].wait()
+                waited.add(needed)
         for pair in range(pairs):
             for side in range(SLABS):
                 line = ((pair % CORES * pairs + pair // CORES * CORES) // CORES * SLABS + side) * parts
-                first = (row * SLABS + side) * columns * parts
+                first = side * columns * parts
                 for part in range(parts):
-                    ready[row, :, line + part, :] = cells_ref[
-                        pair, pl.ds(first + part, columns, stride=parts), :
+                    ready[row, :, line + part, :] = held[
+                        row, pair, pl.ds(first + part, columns, stride=parts), :
                     ]
                 for index in range(columns):
                     place = place_order[row * columns + index]
                     if place != row * columns + index:
-                        slab = (place // columns * SLABS + side) * columns + place % columns
-                        ready[row, index, line : line + parts, :] = cells_ref[
-                            pair, slab * parts : (slab + 1) * parts, :
+                        start = first + place % columns * parts
+                        ready[row, index, line : line + parts, :] = held[
+                            place // columns, pair, start : start + parts, :
                         ]
-        copies.append(
-            pltpu.make_async_copy(
-                ready.at[row], out_ref.at[pl.ds(row * columns, columns)], sems.at[row]
-            )
-        )
-        copies[row].start()
+        copy = pltpu.make_async_copy(
+            ready.at[row], out_ref.at[pl.ds(row * columns, columns)], out_sems.at[row]
+        )
+        copy.start()
+        copies.append(copy)
     for copy in copies:
         copy.wait()
 
@@ -137,7 +153,7 @@
     out_ref[...] = (total[:blocks] + total[blocks:]) / gap_ref[...]
 
 
-def call(kernel, outs, in_memory, cost=None, out_memory=pltpu.VMEM, scratch=()):
+def call(kernel, outs, in_memory, cost=None, out_memory=pltpu.VMEM, scratch=(), vmem_bytes=VMEM_BYTES):
     single = not isinstance(outs, list)
     shapes = [jax.ShapeDtypeStruct(*out) for out in ([outs] if single else outs)]
     specs = [pl.BlockSpec(memory_space=out_memory) for _ in shapes]
@@ -148,7 +164,7 @@
         out_specs=specs[0] if single else specs,
         scratch_shapes=scratch,
         cost_estimate=cost,
-        compiler_params=pltpu.CompilerParams(vmem_limit_bytes=VMEM_BYTES),
+        compiler_params=pltpu.CompilerParams(vmem_limit_bytes=vmem_bytes),
     )
 
 
@@ -205,10 +221,13 @@
     grouped = call(
         functools.partial(regroup_kernel, place_order),
         ((places, lines, VMAX), f32),
-        [vmem],
+        [pltpu.HBM],
         out_memory=pltpu.HBM,
+        vmem_bytes=ALL_VMEM_BYTES,
         scratch=[
+            pltpu.VMEM((rows, pairs, all_lines // rows, VMAX), f32),
             pltpu.VMEM((rows, RING, lines, VMAX), f32),
+            pltpu.SemaphoreType.DMA((rows,)),
             pltpu.SemaphoreType.DMA((rows,)),
         ],
     )(amplitudes.reshape(pairs, all_lines, VMAX))

time: 61.2 us -> 61.1 us (level)
  local copies, waits for them, and re-layouts: 1.68 us -> 0.64 us
  Pallas kernels: 4.21 us -> 5.2 us
    unnamed x8 -> x6, local copies, waits for them, and re-layouts: 1.68 us -> 0.64 us
    pallas_call x1, Pallas kernels: 1 us -> 1.97 us  [body(): call(functools.partial(regroup_kernel, place_order), ((places, lines, VMA...]
  transfers between devices with their start and end apart: 4 -> 4, of which waited for: 1 -> 1; matrix products, arithmetic and copies ran while one was open for 0% -> 0% of each run, Pallas kernels for 4% -> 6%
where the time goes in v7:
time: 61.1 us; the launch traced here: 60.5 us
  starting transfers between devices  27.1 us (44%)
  blocking collectives  21.4 us (35%)
  waiting for transfers between devices  5.44 us (9%)
  Pallas kernels  5.2 us (9%)
  between operations  0.78 us (1%)
  local copies, waits for them, and re-layouts  0.64 us (1%)
    all_to_all x1, blocking collectives, exchange(): lax.all_to_all(blocks_out, ('redist', 'contract'), split_axis=0, concat_a...  21.4 us
    all_to_all x1, starting transfers between devices, exchange(): lax.all_to_all(blocks_out, ('redist', 'contract'), split_axis=0, concat_a...  17.9 us
    ppermute x3, starting transfers between devices, swap(): lax.ppermute(block, axis, [(index, index ^ move) for index in range(count)])  9.15 us
    all_to_all x1, waiting for transfers between devices, exchange(): lax.all_to_all(blocks_out, ('redist', 'contract'), split_axis=0, concat_a...  5.43 us
    pallas_call x1, Pallas kernels, body(): call(functools.partial(regroup_kernel, place_order), ((places, lines, VMA...  1.97 us
  transfers between devices with their start and end apart: 4, of which 1 were waited for; matrix products, arithmetic and copies ran while one was open for 0% of the time, Pallas kernels for 6%

profile of v7, /device:TPU:1, one launch (start us, length us, event | category | flops | bytes accessed | tf_op | source)
XLA Modules:
  0.0 60.5 jit_solution(2181468067604204329)
XLA Ops:
  0.0 4.8 %collective-permute-start = (f32[256,512]{1,0:T(8,128)}, f32[256,512]{1,0:T(8,128)S(1)}, u32[]{:S(2)}, u32[]{:S(2)}) collective-permute-start(f32[256,512]{1,0:T(8,128)} %bitcast.11), channel_id=1, source_target_pairs={{0,64},{8,72},{16,80},{24,88},{32,96},{40,104},{48,112},{56,120},{... | collective-permute-start | bytes 1572872 | tf_op jit(solution)/shard_map/ppermute | solution.py:212
  4.8 2.0 %shard_map.55 = f32[32,32,128]{2,1,0:T(8,128)} custom-call(f32[8,128,128]{2,1,0:T(8,128)} %bitcast.16), custom_call_target="tpu_custom_call" | custom-call | tf_op jit(solution)/shard_map/pallas_call | solution.py:221
  6.8 0.0 copy-start
  6.8 17.9 %all-to-all-start = ((f32[64,16,128]{2,1,0:T(8,128)}), f32[64,16,128]{2,1,0:T(8,128)S(1)}, u32[]{:S(2)}, u32[]{:S(2)}) async-start(f32[64,16,128]{2,1,0:T(8,128)} %bitcast.15), calls=%async_computation | async-start | bytes 1048576 | tf_op jit(solution)/shard_map/all_to_all | solution.py:201
  24.7 0.0 copy-done
  24.8 0.0 copy-start.1
  24.8 2.3 %collective-permute-start.1 = (f32[256,512]{1,0:T(8,128)S(1)}, f32[256,512]{1,0:T(8,128)S(1)}, u32[]{:S(2)}, u32[]{:S(2)}) collective-permute-start(f32[256,512]{1,0:T(8,128)S(1)} %bitcast.12), channel_id=1, source_target_pairs={{0,1},{1,0},{2,3},{3,2},{4,5},{5,4},{6,7},{7,6},{8,9},{9,8},{10,11... | collective-permute-start | bytes 1572872 | tf_op jit(solution)/shard_map/ppermute | solution.py:212
  27.0 0.0 collective-permute-done.refs_1_
  27.1 2.1 %collective-permute-start.2 = (f32[256,512]{1,0:T(8,128)S(1)}, f32[256,512]{1,0:T(8,128)S(1)}, u32[]{:S(2)}, u32[]{:S(2)}) collective-permute-start(f32[256,512]{1,0:T(8,128)S(1)} %collective-permute-done.refs_1_), channel_id=1, source_target_pairs={{0,1},{1,0},{2,3},{3,2},{4,5},{5,4},{6,7},{7,6},{8,9},{9,8},{10,11... | collective-permute-start | bytes 1572872 | tf_op jit(solution)/shard_map/ppermute | solution.py:212
  29.8 0.0 copy-start.2
  29.8 0.0 collective-permute-done.1.refs_2_
  29.8 0.0 copy-done.1
  29.8 0.6 %copy-done.2 = s32[8]{0:T(128)S(1)} copy-done((s32[8]{0:T(128)S(1)}, s32[8]{0:T(128)}, u32[]{:S(2)}) %copy-start.2) | copy-done | bytes 56
  30.4 0.9 %shard_map.56 = (bf16[768,512]{1,0:T(8,128)(2,1)S(1)}, bf16[768,512]{1,0:T(8,128)(2,1)S(1)}, f32[4,128]{1,0:T(4,128)S(1)}) custom-call(s32[8]{0:T(128)S(1)} %copy-done.2, f32[1]{0:T(128)S(6)} %copy.6.pair_energy_ref, f32[4,128]{1,0:T(4,128)S(1)} %bitcast.14, f32[256,512]{1,0:T(8,128)S(1)} %bitcast.13, f32[256,512]{1,0:T(8,128)S(1)} %collective-permute-done.refs_1_, ...), custom_call_target="tpu_custom_call" | custom-call | flops 3932160 | bytes 3145728 | tf_op jit(solution)/shard_map/pallas_call | solution.py:244
  31.3 0.0 collective-permute-done.2.held_ref
  31.4 0.7 %shard_map.57 = (bf16[256,512]{1,0:T(8,128)(2,1)S(1)}, bf16[256,512]{1,0:T(8,128)(2,1)S(1)}) custom-call(s32[8]{0:T(128)S(1)} %copy-done.2, f32[256,512]{1,0:T(8,128)S(1)} %collective-permute-done.2.held_ref), custom_call_target="tpu_custom_call" | custom-call | flops 1310720 | bytes 1048576 | tf_op jit(solution)/shard_map/pallas_call | solution.py:251
  32.0 5.4 %all-to-all-done = f32[64,16,128]{2,1,0:T(8,128)S(1)} async-done(((f32[64,16,128]{2,1,0:T(8,128)}), f32[64,16,128]{2,1,0:T(8,128)S(1)}, u32[]{:S(2)}, u32[]{:S(2)}) %all-to-all-start) | async-done | bytes 524320 | tf_op jit(solution)/shard_map/all_to_all | solution.py:201
  37.5 1.0 %shard_map.58 = f32[32,16,128]{2,1,0:T(8,128)S(1)} custom-call(f32[32,32,128]{2,1,0:T(8,128)S(1)} %bitcast.8, bf16[768,512]{1,0:T(8,128)(2,1)S(1)} %get-tuple-element.10.high_ref, bf16[768,512]{1,0:T(8,128)(2,1)S(1)} %get-tuple-element.11.low_ref, bf16[256,512]{1,0:T(8,128)(2,1)S(1)} %get-tuple-element.12.last_high_ref, ...), custom_call_target="tpu_custom_call" | custom-call | tf_op jit(solution)/shard_map/pallas_call | solution.py:255
  38.5 21.4 %all_to_all.10 = f32[128,4,128]{2,1,0:T(4,128)S(1)} all-to-all(f32[128,4,128]{2,1,0:T(4,128)S(1)} %bitcast.10), channel_id=1, replica_groups={{356,354,352,358,12,10,8,14,20,18,16,22,28,26,24,30,36,34,32,38,44,42,4..., dimensions={0} | all-to-all | bytes 524288 | tf_op jit(solution)/shard_map/all_to_all | solution.py:201
  59.9 0.6 %shard_map.59 = f32[4,128]{1,0:T(4,128)} custom-call(f32[512,128]{1,0:T(8,128)S(1)} %bitcast.9, f32[4,128]{1,0:T(4,128)S(1)} %get-tuple-element.14.gap_ref), custom_call_target="tpu_custom_call" | custom-call | tf_op jit(solution)/shard_map/pallas_call | solution.py:261
Async XLA Ops:
  0.0 27.0 %collective-permute-start = (f32[256,512]{1,0:T(8,128)}, f32[256,512]{1,0:T(8,128)S(1)}, u32[]{:S(2)}, u32[]{:S(2)}) collective-permute-start(f32[256,512]{1,0:T(8,128)} %bitcast.11), channel_id=1, source_target_pairs={{0,64},{8,72},{16,80},{24,88},{32,96},{40,104},{48,112},{56,120},{... | collective-permute-start | bytes 1572872 | tf_op jit(solution)/shard_map/ppermute | solution.py:212
  6.8 17.9 %copy-start = (f32[1,256,512]{2,1,0:T(8,128)S(1)}, f32[1,256,512]{2,1,0:T(8,128)}, u32[]{:S(2)}) copy-start(f32[1,256,512]{2,1,0:T(8,128)} %param.6) | copy-start | bytes 1572868
  6.8 30.7 %all-to-all-start = ((f32[64,16,128]{2,1,0:T(8,128)}), f32[64,16,128]{2,1,0:T(8,128)S(1)}, u32[]{:S(2)}, u32[]{:S(2)}) async-start(f32[64,16,128]{2,1,0:T(8,128)} %bitcast.15), calls=%async_computation | async-start | bytes 1048576 | tf_op jit(solution)/shard_map/all_to_all | solution.py:201
  24.8 5.0 %copy-start.1 = (f32[512]{0:T(512)S(1)}, f32[512]{0:T(512)}, u32[]{:S(2)}) copy-start(f32[512]{0:T(512)} %param.9) | copy-start | bytes 6148
  24.8 5.0 %collective-permute-start.1 = (f32[256,512]{1,0:T(8,128)S(1)}, f32[256,512]{1,0:T(8,128)S(1)}, u32[]{:S(2)}, u32[]{:S(2)}) collective-permute-start(f32[256,512]{1,0:T(8,128)S(1)} %bitcast.12), channel_id=1, source_target_pairs={{0,1},{1,0},{2,3},{3,2},{4,5},{5,4},{6,7},{7,6},{8,9},{9,8},{10,11... | collective-permute-start | bytes 1572872 | tf_op jit(solution)/shard_map/ppermute | solution.py:212
  27.1 4.3 %collective-permute-start.2 = (f32[256,512]{1,0:T(8,128)S(1)}, f32[256,512]{1,0:T(8,128)S(1)}, u32[]{:S(2)}, u32[]{:S(2)}) collective-permute-start(f32[256,512]{1,0:T(8,128)S(1)} %collective-permute-done.refs_1_), channel_id=1, source_target_pairs={{0,1},{1,0},{2,3},{3,2},{4,5},{5,4},{6,7},{7,6},{8,9},{9,8},{10,11... | collective-permute-start | bytes 1572872 | tf_op jit(solution)/shard_map/ppermute | solution.py:212
  29.8 0.7 %copy-start.2 = (s32[8]{0:T(128)S(1)}, s32[8]{0:T(128)}, u32[]{:S(2)}) copy-start(s32[8]{0:T(128)} %count_ref.3) | copy-start | bytes 100

commit v8 on v7

--- a/solution.py
+++ b/solution.py
@@ -184,7 +184,7 @@
         return slab * owners + chip * CORES + core
 
     rows = places // RING
-    place_order = first_swapped(places, rows // 2 * RING + RING // 2)
+    place_order = first_swapped(places, rows // 2 * RING + RING // 2 - 1)
     chip_order = first_swapped(chips, chips // 2)
     same_chip = [
         [device(place, side, chip, core) for place in place_order for core in range(CORES)]

time: 61.1 us -> 63.2 us (1.034)
  waiting for transfers between devices: 5.44 us -> 7.3 us
    all_to_all x1, waiting for transfers between devices: 5.43 us -> 7.29 us  [exchange(): lax.all_to_all(blocks_out, ('redist', 'contract'), split_axis=0, concat_a...]
where the time goes in v8:
time: 63.2 us; the launch traced here: 62.9 us
  starting transfers between devices  27.1 us (43%)
  blocking collectives  21.9 us (35%)
  waiting for transfers between devices  7.3 us (12%)
  Pallas kernels  5.19 us (8%)
  between operations  0.78 us (1%)
  local copies, waits for them, and re-layouts  0.64 us (1%)
    all_to_all x1, blocking collectives, exchange(): lax.all_to_all(blocks_out, ('redist', 'contract'), split_axis=0, concat_a...  21.9 us
    all_to_all x1, starting transfers between devices, exchange(): lax.all_to_all(blocks_out, ('redist', 'contract'), split_axis=0, concat_a...  17.9 us
    ppermute x3, starting transfers between devices, swap(): lax.ppermute(block, axis, [(index, index ^ move) for index in range(count)])  9.15 us
    all_to_all x1, waiting for transfers between devices, exchange(): lax.all_to_all(blocks_out, ('redist', 'contract'), split_axis=0, concat_a...  7.29 us
    pallas_call x1, Pallas kernels, body(): call(functools.partial(regroup_kernel, place_order), ((places, lines, VMA...  1.97 us
  transfers between devices with their start and end apart: 4, of which 1 were waited for; matrix products, arithmetic and copies ran while one was open for 0% of the time, Pallas kernels for 6%

profile of v8, /device:TPU:1, one launch (start us, length us, event | category | flops | bytes accessed | tf_op | source)
XLA Modules:
  0.0 62.9 jit_solution(10770031003831924280)
XLA Ops:
  0.0 4.8 %collective-permute-start = (f32[256,512]{1,0:T(8,128)}, f32[256,512]{1,0:T(8,128)S(1)}, u32[]{:S(2)}, u32[]{:S(2)}) collective-permute-start(f32[256,512]{1,0:T(8,128)} %bitcast.11), channel_id=1, source_target_pairs={{0,64},{8,72},{16,80},{24,88},{32,96},{40,104},{48,112},{56,120},{... | collective-permute-start | bytes 1572872 | tf_op jit(solution)/shard_map/ppermute | solution.py:212
  4.8 2.0 %shard_map.55 = f32[32,32,128]{2,1,0:T(8,128)} custom-call(f32[8,128,128]{2,1,0:T(8,128)} %bitcast.16), custom_call_target="tpu_custom_call" | custom-call | tf_op jit(solution)/shard_map/pallas_call | solution.py:221
  6.8 0.0 copy-start
  6.8 17.9 %all-to-all-start = ((f32[64,16,128]{2,1,0:T(8,128)}), f32[64,16,128]{2,1,0:T(8,128)S(1)}, u32[]{:S(2)}, u32[]{:S(2)}) async-start(f32[64,16,128]{2,1,0:T(8,128)} %bitcast.15), calls=%async_computation | async-start | bytes 1048576 | tf_op jit(solution)/shard_map/all_to_all | solution.py:201
  24.7 0.0 copy-done
  24.7 0.0 copy-start.1
  24.8 2.3 %collective-permute-start.1 = (f32[256,512]{1,0:T(8,128)S(1)}, f32[256,512]{1,0:T(8,128)S(1)}, u32[]{:S(2)}, u32[]{:S(2)}) collective-permute-start(f32[256,512]{1,0:T(8,128)S(1)} %bitcast.12), channel_id=1, source_target_pairs={{0,1},{1,0},{2,3},{3,2},{4,5},{5,4},{6,7},{7,6},{8,9},{9,8},{10,11... | collective-permute-start | bytes 1572872 | tf_op jit(solution)/shard_map/ppermute | solution.py:212
  27.0 0.0 collective-permute-done.refs_1_
  27.0 2.1 %collective-permute-start.2 = (f32[256,512]{1,0:T(8,128)S(1)}, f32[256,512]{1,0:T(8,128)S(1)}, u32[]{:S(2)}, u32[]{:S(2)}) collective-permute-start(f32[256,512]{1,0:T(8,128)S(1)} %collective-permute-done.refs_1_), channel_id=1, source_target_pairs={{0,1},{1,0},{2,3},{3,2},{4,5},{5,4},{6,7},{7,6},{8,9},{9,8},{10,11... | collective-permute-start | bytes 1572872 | tf_op jit(solution)/shard_map/ppermute | solution.py:212
  29.8 0.0 copy-start.2
  29.8 0.0 collective-permute-done.1.refs_2_
  29.8 0.0 copy-done.1
  29.8 0.6 copy-done.2
  30.4 0.9 %shard_map.56 = (bf16[768,512]{1,0:T(8,128)(2,1)S(1)}, bf16[768,512]{1,0:T(8,128)(2,1)S(1)}, f32[4,128]{1,0:T(4,128)S(1)}) custom-call(s32[8]{0:T(128)S(1)} %copy-done.2, f32[1]{0:T(128)S(6)} %copy.6.pair_energy_ref, f32[4,128]{1,0:T(4,128)S(1)} %bitcast.14, f32[256,512]{1,0:T(8,128)S(1)} %bitcast.13, f32[256,512]{1,0:T(8,128)S(1)} %collective-permute-done.refs_1_, ...), custom_call_target="tpu_custom_call" | custom-call | flops 3932160 | bytes 3145728 | tf_op jit(solution)/shard_map/pallas_call | solution.py:244
  31.3 0.0 collective-permute-done.2.held_ref
  31.3 0.7 %shard_map.57 = (bf16[256,512]{1,0:T(8,128)(2,1)S(1)}, bf16[256,512]{1,0:T(8,128)(2,1)S(1)}) custom-call(s32[8]{0:T(128)S(1)} %copy-done.2, f32[256,512]{1,0:T(8,128)S(1)} %collective-permute-done.2.held_ref), custom_call_target="tpu_custom_call" | custom-call | flops 1310720 | bytes 1048576 | tf_op jit(solution)/shard_map/pallas_call | solution.py:251
  32.0 7.3 %all-to-all-done = f32[64,16,128]{2,1,0:T(8,128)S(1)} async-done(((f32[64,16,128]{2,1,0:T(8,128)}), f32[64,16,128]{2,1,0:T(8,128)S(1)}, u32[]{:S(2)}, u32[]{:S(2)}) %all-to-all-start) | async-done | bytes 524320 | tf_op jit(solution)/shard_map/all_to_all | solution.py:201
  39.3 1.0 %shard_map.58 = f32[32,16,128]{2,1,0:T(8,128)S(1)} custom-call(f32[32,32,128]{2,1,0:T(8,128)S(1)} %bitcast.8, bf16[768,512]{1,0:T(8,128)(2,1)S(1)} %get-tuple-element.10.high_ref, bf16[768,512]{1,0:T(8,128)(2,1)S(1)} %get-tuple-element.11.low_ref, bf16[256,512]{1,0:T(8,128)(2,1)S(1)} %get-tuple-element.12.last_high_ref, ...), custom_call_target="tpu_custom_call" | custom-call | tf_op jit(solution)/shard_map/pallas_call | solution.py:255
  40.3 21.9 %all_to_all.10 = f32[128,4,128]{2,1,0:T(4,128)S(1)} all-to-all(f32[128,4,128]{2,1,0:T(4,128)S(1)} %bitcast.10), channel_id=1, replica_groups={{348,346,344,350,12,10,8,14,20,18,16,22,28,26,24,30,36,34,32,38,44,42,4..., dimensions={0} | all-to-all | bytes 524288 | tf_op jit(solution)/shard_map/all_to_all | solution.py:201
  62.2 0.6 %shard_map.59 = f32[4,128]{1,0:T(4,128)} custom-call(f32[512,128]{1,0:T(8,128)S(1)} %bitcast.9, f32[4,128]{1,0:T(4,128)S(1)} %get-tuple-element.14.gap_ref), custom_call_target="tpu_custom_call" | custom-call | tf_op jit(solution)/shard_map/pallas_call | solution.py:261
Async XLA Ops:
  0.0 27.0 %collective-permute-start = (f32[256,512]{1,0:T(8,128)}, f32[256,512]{1,0:T(8,128)S(1)}, u32[]{:S(2)}, u32[]{:S(2)}) collective-permute-start(f32[256,512]{1,0:T(8,128)} %bitcast.11), channel_id=1, source_target_pairs={{0,64},{8,72},{16,80},{24,88},{32,96},{40,104},{48,112},{56,120},{... | collective-permute-start | bytes 1572872 | tf_op jit(solution)/shard_map/ppermute | solution.py:212
  6.8 17.9 %copy-start = (f32[1,256,512]{2,1,0:T(8,128)S(1)}, f32[1,256,512]{2,1,0:T(8,128)}, u32[]{:S(2)}) copy-start(f32[1,256,512]{2,1,0:T(8,128)} %param.6) | copy-start | bytes 1572868
  6.8 32.5 %all-to-all-start = ((f32[64,16,128]{2,1,0:T(8,128)}), f32[64,16,128]{2,1,0:T(8,128)S(1)}, u32[]{:S(2)}, u32[]{:S(2)}) async-start(f32[64,16,128]{2,1,0:T(8,128)} %bitcast.15), calls=%async_computation | async-start | bytes 1048576 | tf_op jit(solution)/shard_map/all_to_all | solution.py:201
  24.7 5.0 %copy-start.1 = (f32[512]{0:T(512)S(1)}, f32[512]{0:T(512)}, u32[]{:S(2)}) copy-start(f32[512]{0:T(512)} %param.9) | copy-start | bytes 6148
  24.8 5.0 %collective-permute-start.1 = (f32[256,512]{1,0:T(8,128)S(1)}, f32[256,512]{1,0:T(8,128)S(1)}, u32[]{:S(2)}, u32[]{:S(2)}) collective-permute-start(f32[256,512]{1,0:T(8,128)S(1)} %bitcast.12), channel_id=1, source_target_pairs={{0,1},{1,0},{2,3},{3,2},{4,5},{5,4},{6,7},{7,6},{8,9},{9,8},{10,11... | collective-permute-start | bytes 1572872 | tf_op jit(solution)/shard_map/ppermute | solution.py:212
  27.0 4.3 %collective-permute-start.2 = (f32[256,512]{1,0:T(8,128)S(1)}, f32[256,512]{1,0:T(8,128)S(1)}, u32[]{:S(2)}, u32[]{:S(2)}) collective-permute-start(f32[256,512]{1,0:T(8,128)S(1)} %collective-permute-done.refs_1_), channel_id=1, source_target_pairs={{0,1},{1,0},{2,3},{3,2},{4,5},{5,4},{6,7},{7,6},{8,9},{9,8},{10,11... | collective-permute-start | bytes 1572872 | tf_op jit(solution)/shard_map/ppermute | solution.py:212
  29.8 0.7 %copy-start.2 = (s32[8]{0:T(128)S(1)}, s32[8]{0:T(128)}, u32[]{:S(2)}) copy-start(s32[8]{0:T(128)} %count_ref.3) | copy-start | bytes 100
